TPU v7x, 512 devices: a whole 4x4x16 slice. The times are simulated.
512 devices in a mesh: dp: 128 (over z, y, core), split: 4 (over x).
Axes of the slice: x: 4, y: 4, z: 16, core: 2. Of those that a mesh axis runs over, the one named last changes fastest.
Arguments:
- features: bfloat16 [262144, 1024], P(('dp', 'split')), may hold values from -60 to 60
- proj_weight: bfloat16 [1024, 768], replicated, may hold values from -0.1875 to 0.1875
- row_cluster: int32 [262144], P(('dp', 'split')), may hold values from -1 to 127, as said below
- row_rank: int32 [262144], P(('dp', 'split')), may hold values from -1 to 2047, as said below
- owner_slot: int32 [128], replicated, may hold values from 0 to 127, as said below
- tile_size: int32 [128], replicated, may hold values from 1024 to 2048
Outputs:
- max_sim: float32 [128, 2048], P('dp', 'split')
Inputs may be any that keep to these rules, and one draw needn't show every extreme that they name: Cluster c is named by exactly tile_size[c] rows, whose row_rank values are 0 to tile_size[c] - 1, each once. Grouping named rows by owner_slot[row_cluster] // 1 and row_rank // 512, the 512 rows of one device put at most 1 row into one group, and some group gets exactly 1 from every device. `row_rank`: -1 exactly where row_cluster is -1. A permutation of 0 to 127; cluster c is held by dp index owner_slot[c].
All inputs are finite; a program needn't handle non-finite values.
Results may differ from a plain program's by a relative error of at most 0.0003.
Values may be sent and summed in bfloat16 or wider, within the bound.
No kernel may reach another device: no remote copies, remote signals or barrier semaphores. Data moves between devices by JAX's collectives and lax.ppermute only.
A program may use at most 64 MiB of HBM per device.

v0:
```python
import jax
import jax.numpy as jnp
from jax import lax
from jax.sharding import PartitionSpec as P

TILE = 2048


eps_norm = 1e-06


def earlier_max(best, row_vectors, column_vectors, row_start):
    scores = jnp.einsum(
        "kie,kje->kij", row_vectors, column_vectors, preferred_element_type=jnp.float32
    )
    row_pos = row_start + jnp.arange(row_vectors.shape[1], dtype=jnp.int32)
    column_pos = jnp.arange(column_vectors.shape[1], dtype=jnp.int32)
    earlier = column_pos[None, None, :] < row_pos[None, :, None]
    return jnp.maximum(best, jnp.max(jnp.where(earlier, scores, -1.0), axis=2))


def local(features, proj_weight, row_cluster, row_rank, owner_slot, tile_size):
    dp_count = lax.axis_size("dp")
    split_count = lax.axis_size("split")
    devices = dp_count * split_count
    rows_dev = features.shape[0]
    clusters = owner_slot.shape[0]
    per_owner = clusters // dp_count
    block = TILE // split_count
    capacity = rows_dev // devices
    width = proj_weight.shape[1]
    projected = jnp.dot(features, proj_weight, preferred_element_type=jnp.float32)
    normed = projected * lax.rsqrt(jnp.sum(projected * projected, axis=1, keepdims=True) + eps_norm)
    normed = normed.astype(jnp.bfloat16)
    living = row_cluster >= 0
    matches = row_cluster[:, None] == jnp.arange(clusters, dtype=jnp.int32)[None, :]
    held_slot = jnp.sum(jnp.where(matches, owner_slot[None, :], 0), axis=1)
    receiver = jnp.where(living, held_slot // per_owner * split_count + row_rank // block, devices)
    target = held_slot % per_owner * block + row_rank % block
    row_ids = jnp.arange(rows_dev, dtype=jnp.int32)
    ordering = jnp.argsort(receiver * rows_dev + row_ids)
    sorted_receiver = receiver[ordering]
    group_start = jnp.searchsorted(sorted_receiver, sorted_receiver, side="left")
    placing = jnp.where(
        sorted_receiver < devices,
        sorted_receiver * capacity + row_ids - group_start,
        devices * capacity,
    )
    outgoing = (
        jnp.zeros((devices * capacity, width), jnp.bfloat16)
        .at[placing]
        .set(normed[ordering], mode="drop")
    )
    labels = (
        jnp.full((devices * capacity,), -1, jnp.int32)
        .at[placing]
        .set(target[ordering], mode="drop")
    )
    outgoing = outgoing.reshape(dp_count, split_count, capacity, width)
    labels = labels.reshape(dp_count, split_count, capacity)
    arrived, arrived_labels = (
        lax.all_to_all(
            lax.all_to_all(outgoing, "dp", split_axis=0, concat_axis=0, tiled=True),
            "split",
            split_axis=1,
            concat_axis=1,
            tiled=True,
        ),
        lax.all_to_all(
            lax.all_to_all(labels, "dp", split_axis=0, concat_axis=0, tiled=True),
            "split",
            split_axis=1,
            concat_axis=1,
            tiled=True,
        ),
    )
    arrived = arrived.reshape(devices * capacity, width)
    arrived_labels = arrived_labels.reshape(devices * capacity)
    landing = jnp.where(arrived_labels >= 0, arrived_labels, per_owner * block)
    members = (
        jnp.zeros((per_owner * block, width), jnp.bfloat16).at[landing].set(arrived, mode="drop")
    )
    members = members.reshape(per_owner, block, width)
    block_index = lax.axis_index("split")
    owner_index = lax.axis_index("dp")
    my_slots = owner_index * per_owner + jnp.arange(per_owner, dtype=jnp.int32)
    my_size = jnp.sum(
        jnp.where(owner_slot[None, :] == my_slots[:, None], tile_size[None, :], 0), axis=1
    )
    my_ranks = block_index * block + jnp.arange(block, dtype=jnp.int32)
    best = earlier_max(
        jnp.full((per_owner, block), -1.0, jnp.float32),
        members,
        lax.all_gather(members, "split", axis=1, tiled=True),
        block_index * block,
    )
    return jnp.where(my_ranks[None, :] < my_size[:, None], best, -1.0)


def solution(mesh):
    return jax.shard_map(
        local,
        mesh=mesh,
        in_specs=(P(("dp", "split"), None), P(), P(("dp", "split")), P(("dp", "split")), P(), P()),
        out_specs=P("dp", "split"),
        check_vma=False,
    )
```

profile of v0, /device:TPU:1, one launch (start us, length us, event | category | flops | bytes accessed | tf_op | source)
XLA Modules:
  0.0 225.0 jit_solution(10072618363199853070)
XLA Ops:
  6.5 0.0 copy-start
  6.5 1.0 select_reduce_fusion.1
  7.6 0.7 iota_add_fusion
  8.3 3.8 %sort.17 = (s32[512]{0:T(512)}, s32[512]{0:T(512)S(1)}) sort(s32[512]{0:T(512)S(1)} %get-tuple-element.100, s32[512]{0:T(512)S(1)} %iota.30), dimensions={0}, to_apply=%region_2.3 | sort | flops 4608 | bytes 8192 | tf_op jit(solution)/shard_map/jit(argsort)/sort | solution.py:41
  12.1 3.5 %gather_fusion.1 = s32[512]{0:T(512)S(1)} fusion(s32[512]{0:T(512)S(1)} %get-tuple-element.101, s32[1024]{0:T(1024)S(1)} %pad_clamp_fusion.1), kind=kCustom, calls=%fused_computation.1 | custom fusion | bytes 6144 | tf_op jit(solution)/shard_map/gather | solution.py:42
  15.6 3.5 %gather_fusion.2 = s32[512]{0:T(512)S(1)} fusion(s32[512]{0:T(512)S(1)} %get-tuple-element.102, s32[1024]{0:T(1024)S(1)} %pad_clamp_fusion.1), kind=kCustom, calls=%fused_computation.2 | custom fusion | bytes 6144 | tf_op jit(solution)/shard_map/gather | solution.py:57
  19.1 0.0 copy-start.3
  19.1 35.9 %while.25 = (s32[]{:T(128)}, u32[512]{0:T(512)S(1)}, u32[512]{0:T(512)S(1)}, s32[512]{0:T(512)S(1)}, s32[]{:T(128)}, /*index=5*/s32[]{:T(128)}, s32[]{}) while((s32[]{:T(128)}, u32[512]{0:T(512)S(1)}, u32[512]{0:T(512)S(1)}, s32[512]{0:T(512)S(1)}, s32[]{:T(128)}, /*index=5*/s32[]{:T(128)}, s32[]{}) %tuple.39), condition=%wide.region_4.5_spmd.clone, body=%wide.region_3.4_spmd.clone.sunk | while | flops 10244 | bytes 40037 | solution.py:43
  19.1 3.5 %gather_fusion = s32[512]{0:T(512)S(1)} fusion(s32[512]{0:T(512)S(1)} %get-tuple-element.151, u32[1024]{0:T(1024)S(1)} %pad_clamp_fusion.3), kind=kCustom, calls=%fused_computation.clone.clone.1 | custom fusion | bytes 6144 | tf_op jit(solution)/shard_map/jit(searchsorted)/jit(_searchsorted_scan_impl)/vmap(jit(_searchsorted_scan_impl))/while/body/eval_jaxpr/gather | solution.py:43
  22.7 3.5 %gather_fusion = s32[512]{0:T(512)S(1)} fusion(s32[512]{0:T(512)S(1)} %get-tuple-element.151, u32[1024]{0:T(1024)S(1)} %pad_clamp_fusion.3), kind=kCustom, calls=%fused_computation.clone.clone.1 | custom fusion | bytes 6144 | tf_op jit(solution)/shard_map/jit(searchsorted)/jit(_searchsorted_scan_impl)/vmap(jit(_searchsorted_scan_impl))/while/body/eval_jaxpr/gather | solution.py:43
  26.3 3.5 %gather_fusion = s32[512]{0:T(512)S(1)} fusion(s32[512]{0:T(512)S(1)} %get-tuple-element.151, u32[1024]{0:T(1024)S(1)} %pad_clamp_fusion.3), kind=kCustom, calls=%fused_computation.clone.clone.1 | custom fusion | bytes 6144 | tf_op jit(solution)/shard_map/jit(searchsorted)/jit(_searchsorted_scan_impl)/vmap(jit(_searchsorted_scan_impl))/while/body/eval_jaxpr/gather | solution.py:43
  29.9 3.5 %gather_fusion = s32[512]{0:T(512)S(1)} fusion(s32[512]{0:T(512)S(1)} %get-tuple-element.151, u32[1024]{0:T(1024)S(1)} %pad_clamp_fusion.3), kind=kCustom, calls=%fused_computation.clone.clone.1 | custom fusion | bytes 6144 | tf_op jit(solution)/shard_map/jit(searchsorted)/jit(_searchsorted_scan_impl)/vmap(jit(_searchsorted_scan_impl))/while/body/eval_jaxpr/gather | solution.py:43
  33.5 3.5 %gather_fusion = s32[512]{0:T(512)S(1)} fusion(s32[512]{0:T(512)S(1)} %get-tuple-element.151, u32[1024]{0:T(1024)S(1)} %pad_clamp_fusion.3), kind=kCustom, calls=%fused_computation.clone.clone.1 | custom fusion | bytes 6144 | tf_op jit(solution)/shard_map/jit(searchsorted)/jit(_searchsorted_scan_impl)/vmap(jit(_searchsorted_scan_impl))/while/body/eval_jaxpr/gather | solution.py:43
  37.1 3.5 %gather_fusion = s32[512]{0:T(512)S(1)} fusion(s32[512]{0:T(512)S(1)} %get-tuple-element.151, u32[1024]{0:T(1024)S(1)} %pad_clamp_fusion.3), kind=kCustom, calls=%fused_computation.clone.clone.1 | custom fusion | bytes 6144 | tf_op jit(solution)/shard_map/jit(searchsorted)/jit(_searchsorted_scan_impl)/vmap(jit(_searchsorted_scan_impl))/while/body/eval_jaxpr/gather | solution.py:43
  40.7 3.5 %gather_fusion = s32[512]{0:T(512)S(1)} fusion(s32[512]{0:T(512)S(1)} %get-tuple-element.151, u32[1024]{0:T(1024)S(1)} %pad_clamp_fusion.3), kind=kCustom, calls=%fused_computation.clone.clone.1 | custom fusion | bytes 6144 | tf_op jit(solution)/shard_map/jit(searchsorted)/jit(_searchsorted_scan_impl)/vmap(jit(_searchsorted_scan_impl))/while/body/eval_jaxpr/gather | solution.py:43
  44.3 3.5 %gather_fusion = s32[512]{0:T(512)S(1)} fusion(s32[512]{0:T(512)S(1)} %get-tuple-element.151, u32[1024]{0:T(1024)S(1)} %pad_clamp_fusion.3), kind=kCustom, calls=%fused_computation.clone.clone.1 | custom fusion | bytes 6144 | tf_op jit(solution)/shard_map/jit(searchsorted)/jit(_searchsorted_scan_impl)/vmap(jit(_searchsorted_scan_impl))/while/body/eval_jaxpr/gather | solution.py:43
  47.8 3.5 %gather_fusion = s32[512]{0:T(512)S(1)} fusion(s32[512]{0:T(512)S(1)} %get-tuple-element.151, u32[1024]{0:T(1024)S(1)} %pad_clamp_fusion.3), kind=kCustom, calls=%fused_computation.clone.clone.1 | custom fusion | bytes 6144 | tf_op jit(solution)/shard_map/jit(searchsorted)/jit(_searchsorted_scan_impl)/vmap(jit(_searchsorted_scan_impl))/while/body/eval_jaxpr/gather | solution.py:43
  51.4 3.5 %gather_fusion = s32[512]{0:T(512)S(1)} fusion(s32[512]{0:T(512)S(1)} %get-tuple-element.151, u32[1024]{0:T(1024)S(1)} %pad_clamp_fusion.3), kind=kCustom, calls=%fused_computation.clone.clone.1 | custom fusion | bytes 6144 | tf_op jit(solution)/shard_map/jit(searchsorted)/jit(_searchsorted_scan_impl)/vmap(jit(_searchsorted_scan_impl))/while/body/eval_jaxpr/gather | solution.py:43
  55.0 2.4 %scatter_custom_fusion = s32[512]{0:T(512)S(1)} fusion(s32[512]{0:T(512)S(1)} %compare_select_fusion.3, s32[512]{0:T(512)S(1)} %gather_fusion.2, s32[]{:T(128)} %constant.93.clone.1), kind=kCustom, calls=%fused_computation.43 | custom fusion | bytes 2052 | tf_op jit(solution)/shard_map/scatter | solution.py:57
  57.4 0.7 reshape.102
  58.2 20.6 %all-to-all-start = ((s32[128,4,1]{1,2,0:T(1,128)}), s32[128,4,1]{1,2,0:T(1,128)S(1)}, u32[]{:S(2)}, u32[]{:S(2)}) async-start(s32[128,4,1]{1,2,0:T(1,128)} %bitcast), calls=%async_computation | async-start | bytes 131072 | tf_op jit(solution)/shard_map/all_to_all | solution.py:70
  78.8 1.1 multiply_reduce_fusion
  79.8 0.2 multiply_convert_fusion
  80.0 5.8 %scatter_custom_fusion.1 = bf16[512,768]{1,0:T(8,128)(2,1)S(1)} fusion(s32[512]{0:T(512)S(1)} %compare_select_fusion.3, bf16[512,768]{1,0:T(8,128)(2,1)S(1)} %multiply_convert_fusion, s32[1024]{0:T(1024)S(1)} %pad_clamp_fusion.1, bf16[]{:T(256)} %constant.92.clone.1), kind=kCustom, calls=%fused_computation.15 | custom fusion | bytes 786434 | tf_op jit(solution)/shard_map/scatter | solution.py:52
  85.8 1.1 reshape.104
  86.9 6.7 %all-to-all-done = s32[128,4,1]{1,2,0:T(1,128)S(1)} async-done(((s32[128,4,1]{1,2,0:T(1,128)}), s32[128,4,1]{1,2,0:T(1,128)S(1)}, u32[]{:S(2)}, u32[]{:S(2)}) %all-to-all-start) | async-done | bytes 2080 | tf_op jit(solution)/shard_map/all_to_all | solution.py:70
  93.6 9.6 %all-to-all-start.2 = ((bf16[128,4,1,768]{3,1,2,0:T(4,128)(2,1)}), bf16[128,4,1,768]{3,1,2,0:T(4,128)(2,1)S(1)}, u32[]{:S(2)}, u32[]{:S(2)}) async-start(bf16[128,4,1,768]{3,1,2,0:T(4,128)(2,1)} %reshape.104), calls=%async_computation.2 | async-start | bytes 1572864 | tf_op jit(solution)/shard_map/all_to_all | solution.py:63
  103.2 0.7 copy.17
  103.8 40.8 %all-to-all-done.2 = bf16[128,4,1,768]{3,1,2,0:T(4,128)(2,1)S(1)} async-done(((bf16[128,4,1,768]{3,1,2,0:T(4,128)(2,1)}), bf16[128,4,1,768]{3,1,2,0:T(4,128)(2,1)S(1)}, u32[]{:S(2)}, u32[]{:S(2)}) %all-to-all-start.2) | async-done | bytes 786464 | tf_op jit(solution)/shard_map/all_to_all | solution.py:63
  144.6 4.0 %all-to-all-start.1 = ((s32[128,4,1]{0,2,1:T(1,128)}), s32[128,4,1]{0,2,1:T(1,128)S(1)}, u32[]{:S(2)}, u32[]{:S(2)}) async-start(s32[128,4,1]{0,2,1:T(1,128)} %copy.17), calls=%async_computation.1 | async-start | bytes 4096 | tf_op jit(solution)/shard_map/all_to_all | solution.py:69
  148.6 1.0 copy.19
  149.6 3.1 %all-to-all-done.1 = s32[128,4,1]{0,2,1:T(1,128)S(1)} async-done(((s32[128,4,1]{0,2,1:T(1,128)}), s32[128,4,1]{0,2,1:T(1,128)S(1)}, u32[]{:S(2)}, u32[]{:S(2)}) %all-to-all-start.1) | async-done | bytes 2080 | tf_op jit(solution)/shard_map/all_to_all | solution.py:69
  152.6 3.5 %all-to-all-start.3 = ((bf16[128,4,1,768]{3,0,2,1:T(8,128)(2,1)}), bf16[128,4,1,768]{3,0,2,1:T(8,128)(2,1)S(1)}, u32[]{:S(2)}, u32[]{:S(2)}) async-start(bf16[128,4,1,768]{3,0,2,1:T(8,128)(2,1)} %copy.19), calls=%async_computation.3 | async-start | bytes 1572864 | tf_op jit(solution)/shard_map/all_to_all | solution.py:62
  156.1 0.0 all-gather.3.cloned.1.call-start
  156.2 0.1 copy.18
  156.3 0.1 reshape.103
  156.4 8.5 %all-to-all-done.3 = bf16[128,4,1,768]{3,0,2,1:T(8,128)(2,1)S(1)} async-done(((bf16[128,4,1,768]{3,0,2,1:T(8,128)(2,1)}), bf16[128,4,1,768]{3,0,2,1:T(8,128)(2,1)S(1)}, u32[]{:S(2)}, u32[]{:S(2)}) %all-to-all-start.3) | async-done | bytes 786464 | tf_op jit(solution)/shard_map/all_to_all | solution.py:62
  164.9 0.6 copy.20
  165.5 0.0 copy-start.1
  165.5 0.0 copy-start.2
  165.6 0.2 reshape.160
  165.7 3.6 %scatter_custom_fusion.2 = bf16[512,768]{1,0:T(8,128)(2,1)} fusion(s32[512]{0:T(512)S(1)} %bitcast.15, bf16[512,768]{1,0:T(8,128)(2,1)S(1)} %reshape.160, bf16[]{:T(256)} %constant.92.clone.1), kind=kCustom, calls=%fused_computation.17 | custom fusion | bytes 786434 | tf_op jit(solution)/shard_map/scatter | solution.py:81
  169.3 0.0 all-gather.3.cloned.1.call-update
  169.3 0.0 copy-done.1
  169.4 0.7 fusion.10
  170.0 42.9 %all-gather.3.cloned.1.call-done = bf16[2048,768]{1,0:T(8,128)(2,1)} async-done(((bf16[512,768]{1,0:T(8,128)(2,1)}), bf16[2048,768]{1,0:T(8,128)(2,1)}) %all-gather.3.cloned.1.call-update) | async-done | bytes 3145744 | tf_op jit(solution)/shard_map/all_gather | solution.py:94
  212.9 4.0 %select_reduce_fusion = f32[512]{0:T(512)S(1)} fusion(bf16[512,768]{1,0:T(8,128)(2,1)} %scatter_custom_fusion.2, bf16[2048,768]{1,0:T(8,128)(2,1)} %all-gather.3.cloned.1.call-done, s32[512]{0:T(512)S(1)} %iota_add_fusion.1), kind=kOutput, calls=%fused_computation.11 | convolution fusion | flops 1613757952 | bytes 3936256 | tf_op jit(solution)/shard_map/kie,kje->kij/dot_general | solution.py:13
  217.0 1.2 compare_select_fusion.2
  (63 shorter events, 0.5 us)
Async XLA Ops:
  6.5 72.2 %copy-start = (bf16[1024,768]{1,0:T(8,128)(2,1)S(1)}, bf16[1024,768]{1,0:T(8,128)(2,1)}, u32[]{:S(2)}) copy-start(bf16[1024,768]{1,0:T(8,128)(2,1)} %param.9) | copy-start | bytes 4718596
  19.1 59.7 %copy-start.3 = (bf16[512,1024]{1,0:T(8,128)(2,1)S(1)}, bf16[512,1024]{1,0:T(8,128)(2,1)}, u32[]{:S(2)}) copy-start(bf16[512,1024]{1,0:T(8,128)(2,1)} %param.8) | copy-start | bytes 3145732
  58.2 35.4 %all-to-all-start = ((s32[128,4,1]{1,2,0:T(1,128)}), s32[128,4,1]{1,2,0:T(1,128)S(1)}, u32[]{:S(2)}, u32[]{:S(2)}) async-start(s32[128,4,1]{1,2,0:T(1,128)} %bitcast), calls=%async_computation | async-start | bytes 131072 | tf_op jit(solution)/shard_map/all_to_all | solution.py:70
  93.6 51.0 %all-to-all-start.2 = ((bf16[128,4,1,768]{3,1,2,0:T(4,128)(2,1)}), bf16[128,4,1,768]{3,1,2,0:T(4,128)(2,1)S(1)}, u32[]{:S(2)}, u32[]{:S(2)}) async-start(bf16[128,4,1,768]{3,1,2,0:T(4,128)(2,1)} %reshape.104), calls=%async_computation.2 | async-start | bytes 1572864 | tf_op jit(solution)/shard_map/all_to_all | solution.py:63
  144.6 8.0 %all-to-all-start.1 = ((s32[128,4,1]{0,2,1:T(1,128)}), s32[128,4,1]{0,2,1:T(1,128)S(1)}, u32[]{:S(2)}, u32[]{:S(2)}) async-start(s32[128,4,1]{0,2,1:T(1,128)} %copy.17), calls=%async_computation.1 | async-start | bytes 4096 | tf_op jit(solution)/shard_map/all_to_all | solution.py:69
  152.6 12.3 %all-to-all-start.3 = ((bf16[128,4,1,768]{3,0,2,1:T(8,128)(2,1)}), bf16[128,4,1,768]{3,0,2,1:T(8,128)(2,1)S(1)}, u32[]{:S(2)}, u32[]{:S(2)}) async-start(bf16[128,4,1,768]{3,0,2,1:T(8,128)(2,1)} %copy.19), calls=%async_computation.3 | async-start | bytes 1572864 | tf_op jit(solution)/shard_map/all_to_all | solution.py:62
  156.1 56.8 %all-gather.3.cloned.1.call-start = ((), (), s32[]{:S(2)}) async-start(), calls=%async_computation.4 | async-start | bytes 3932160 | tf_op jit(solution)/shard_map/all_gather | solution.py:94
  165.5 3.8 %copy-start.1 = (s32[128]{0:T(128)S(1)}, s32[128]{0:T(128)}, u32[]{:S(2)}) copy-start(s32[128]{0:T(128)} %param.12) | copy-start | bytes 1540
  165.5 3.8 %copy-start.2 = (s32[128]{0:T(128)S(1)}, s32[128]{0:T(128)}, u32[]{:S(2)}) copy-start(s32[128]{0:T(128)} %param.13) | copy-start | bytes 1540
Sparse Core Ops, SparseCore 0:
  169.4 43.4 all-gather.2
where the time goes:
time: 225 us
  waiting for transfers between devices  102 us (45%)
  local copies, waits for them, and re-layouts  58.1 us (26%)
  starting transfers between devices  37.7 us (17%)
  between operations  13.6 us (6%)
  other arithmetic  8 us (4%)
  matrix products  5.12 us (2%)
    all_gather x1, waiting for transfers between devices, local(): lax.all_gather(members, 'split', axis=1, tiled=True)  42.9 us
    all_to_all x1, waiting for transfers between devices, local(): lax.all_to_all(outgoing, 'dp', split_axis=0, concat_axis=0, tiled=True)  40.8 us
    gather x10, local copies, waits for them, and re-layouts, local(): jnp.searchsorted(sorted_receiver, sorted_receiver, side='left')  34.9 us
    all_to_all x1, starting transfers between devices, local(): lax.all_to_all(labels, 'dp', split_axis=0, concat_axis=0, tiled=True)  20.6 us
    all_to_all x1, starting transfers between devices, local(): lax.all_to_all(outgoing, 'dp', split_axis=0, concat_axis=0, tiled=True)  9.58 us
    all_to_all x1, waiting for transfers between devices, local(): lax.all_to_all(lax.all_to_all(outgoing, 'dp', split_axis=0, concat_axis=0...  8.51 us
    all_to_all x1, waiting for transfers between devices, local(): lax.all_to_all(labels, 'dp', split_axis=0, concat_axis=0, tiled=True)  6.71 us
    scatter x1, local copies, waits for them, and re-layouts, local(): outgoing = jnp.zeros((devices * capacity, width), jnp.bfloat16).at[placin...  5.8 us
  transfers between devices with their start and end apart: 5, of which 5 were waited for; matrix products, arithmetic and copies ran while one was open for 5% of the time, Pallas kernels for 0%

commit v1 on v0

v1 whole, which is shorter than its diff:
```python
import jax
import jax.numpy as jnp
from jax import lax
from jax.experimental import pallas as pl
from jax.experimental.pallas import tpu as pltpu
from jax.sharding import PartitionSpec as P

TILE = 2048
EPS = 1e-06
AXES = ("dp", "split")
NT = (((1,), (1,)), ((), ()))
TN = (((0,), (0,)), ((), ()))


def iota(shape, dim):
    return lax.broadcasted_iota(jnp.int32, shape, dim)


def bf16(mask_or_int):
    return mask_or_int.astype(jnp.float32).astype(jnp.bfloat16)


def project_kernel(splits, block, features_ref, weight_ref, cluster_ref, rank_ref, owner_ref, out_ref):
    cluster, rank = cluster_ref[...], rank_ref[...]
    clusters, rows, width = owner_ref.shape[1], cluster.shape[1], weight_ref.shape[1]
    projected = jnp.dot(features_ref[...], weight_ref[...], preferred_element_type=jnp.float32)
    normed = projected * lax.rsqrt(jnp.sum(projected * projected, axis=1, keepdims=True) + EPS)
    normed = normed.astype(jnp.bfloat16)

    owner = bf16(jnp.broadcast_to(owner_ref[...], (8, clusters)))
    named = bf16(iota((clusters, rows), 0) == cluster)
    slot = jnp.dot(owner, named, preferred_element_type=jnp.float32)[0:1].astype(jnp.int32)
    place = jnp.where(cluster >= 0, slot * splits + rank // block, -1)
    high, low = (rank + 1) // 16, (rank + 1) % 16
    lane = iota((128, rows), 0)
    numbers = jnp.zeros((rows // 2, 128), jnp.float32)
    for i in range(2):
        chosen = bf16(2 * iota((rows // 2, rows), 0) + i == place)
        sent = jnp.dot(chosen, normed, preferred_element_type=jnp.float32)
        out_ref[:, i * width : (i + 1) * width] = sent.astype(jnp.bfloat16)
        digits = bf16(jnp.where(lane == 2 * i, high, jnp.where(lane == 2 * i + 1, low, 0)))
        numbers += lax.dot_general(chosen, digits, NT, preferred_element_type=jnp.float32)
    out_ref[:, 2 * width :] = numbers.astype(jnp.bfloat16)


def gram_kernel(width, index_ref, owner_ref, size_ref, *refs):
    out_ref = refs[-1]
    block = out_ref.shape[1]
    start = index_ref[1] * block
    rank = start + iota((1, block), 1)
    number = (rank + 1).astype(jnp.float32)
    parts = []
    mine = jnp.zeros((block, width), jnp.float32)
    for ref in refs[:-1]:
        rows = jnp.concatenate([ref[:, :width], ref[:, width : 2 * width]], axis=0)
        digits = ref[:, 2 * width :].astype(jnp.float32)
        label = jnp.concatenate([digits[:, i : i + 1] * 16 + digits[:, i + 1 : i + 2] for i in (0, 2)], axis=0)
        chosen = bf16(label == number)
        mine += lax.dot_general(chosen, rows, TN, preferred_element_type=jnp.float32)
        parts.append((rows, label))
    mine = mine.astype(jnp.bfloat16)
    best = jnp.full((8, block), -1.0, jnp.float32)
    for rows, label in parts:
        scores = lax.dot_general(rows, mine, NT, preferred_element_type=jnp.float32)
        scores = jnp.where((label > 0) & (label < number), scores, -1.0)
        best = jnp.maximum(best, jnp.max(scores.reshape(-1, 8, block), axis=0))
    best = jnp.max(best, axis=0, keepdims=True)
    size = jnp.sum(jnp.where(owner_ref[...] == index_ref[0], size_ref[...], 0), axis=1, keepdims=True)
    out_ref[...] = jnp.where(rank < size, best, -1.0)


def local(features, proj_weight, row_cluster, row_rank, owner_slot, tile_size):
    owners, splits = lax.axis_size("dp"), lax.axis_size("split")
    planes = owners // (2 * splits)
    rows, width = features.shape[0], proj_weight.shape[1]
    block = TILE // splits
    vmem = pl.BlockSpec(memory_space=pltpu.VMEM)
    smem = pl.BlockSpec(memory_space=pltpu.SMEM)
    params = pltpu.CompilerParams(vmem_limit_bytes=40 * 1024 * 1024)
    owner_row = owner_slot.reshape(1, -1)

    def device(z, y, core, x):
        return ((z * splits + y) * 2 + core) * splits + x

    everywhere = [(z, a, b) for z in range(planes) for a in range(splits) for b in range(splits)]
    diagonals = [
        [
            device(z, (g - j) % splits, 1, j) if core else device(z, j, 0, (g - j) % splits)
            for z in range(planes)
            for j in range(splits)
            for core in range(2)
        ]
        for g in range(splits)
    ]

    def shift(array, step):
        pairs = [(device(z, a, 0, b), device(z, a, 0, (b + step) % splits)) for z, a, b in everywhere]
        pairs += [(device(z, a, 1, b), device(z, (a + step) % splits, 1, b)) for z, a, b in everywhere]
        return lax.ppermute(array, AXES, pairs)

    outgoing = pl.pallas_call(
        lambda *refs: project_kernel(splits, block, *refs),
        out_shape=jax.ShapeDtypeStruct((rows // 2, 2 * width + 128), jnp.bfloat16),
        in_specs=[vmem] * 5,
        out_specs=vmem,
        compiler_params=params,
        name="project",
    )(features, proj_weight, row_cluster.reshape(1, rows), row_rank.reshape(1, rows), owner_row)

    own = lax.all_to_all(
        outgoing.reshape(owners, splits // 2, -1), AXES, 0, 0, tiled=True, axis_index_groups=diagonals
    ).reshape(rows // 2, -1)
    first, second = own[: rows // 4], own[rows // 4 :]
    left_first, right_second = shift(first, 1), shift(second, -1)
    left_second, right_first = shift(second, 1), shift(first, -1)
    far_first, far_second = shift(left_first, 1), shift(right_second, -1)

    owner, x = lax.axis_index("dp"), lax.axis_index("split")
    z, y, core = owner // (2 * splits), owner // 2 % splits, owner % 2
    index = jnp.stack(
        [jnp.where(core == 0, owner, (z * splits + x) * 2 + 1), jnp.where(core == 0, x, y)]
    ).astype(jnp.int32)
    best = pl.pallas_call(
        lambda *refs: gram_kernel(width, *refs),
        out_shape=jax.ShapeDtypeStruct((1, block), jnp.float32),
        in_specs=[smem] + [vmem] * 9,
        out_specs=vmem,
        compiler_params=params,
        name="gram",
    )(index, owner_row, tile_size.reshape(1, -1), own, left_first, right_second, left_second, right_first, far_first, far_second)
    home = [(device(z, a, 0, b), device(z, a, 0, b)) for z, a, b in everywhere]
    home += [(device(z, a, 1, b), device(z, b, 1, a)) for z, a, b in everywhere]
    return lax.ppermute(best, AXES, home)


def solution(mesh):
    return jax.shard_map(
        local,
        mesh=mesh,
        in_specs=(P(("dp", "split"), None), P(), P(("dp", "split")), P(("dp", "split")), P(), P()),
        out_specs=P("dp", "split"),
        check_vma=False,
    )
```

time: 225 us -> 119 us (0.53)
  the two profiles are of different devices: /device:TPU:1 before, /device:TPU:7 now
where the time goes in v1:
time: 119 us; the launch traced here: 118 us
  blocking collectives  71.4 us (60%)
  starting transfers between devices  20.2 us (17%)
  local copies, waits for them, and re-layouts  10.7 us (9%)
  waiting for transfers between devices  8.39 us (7%)
  Pallas kernels  7.5 us (6%)
    all_to_all x1, blocking collectives, local(): lax.all_to_all(outgoing.reshape(owners, splits // 2, -1), AXES, 0, 0, til...  71.4 us
    ppermute x6, starting transfers between devices, shift(): return lax.ppermute(array, AXES, pairs)  18.2 us
    ppermute x1, waiting for transfers between devices, local(): return lax.ppermute(best, AXES, home)  5.64 us
    unnamed x17, local copies, waits for them, and re-layouts  5.55 us
    pallas_call x1, Pallas kernels, local(): pl.pallas_call(lambda *refs: gram_kernel(width, *refs), out_shape=jax.Sha...  5.47 us
    ppermute x6, waiting for transfers between devices, shift(): return lax.ppermute(array, AXES, pairs)  2.75 us
    slice x3, local copies, waits for them, and re-layouts, local(): first, second = (own[:rows // 4], own[rows // 4:])  2.43 us
  transfers between devices with their start and end apart: 7, of which 2 were waited for; matrix products, arithmetic and copies ran while one was open for 3% of the time, Pallas kernels for 0%

profile of v1, /device:TPU:7, one launch (start us, length us, event | category | flops | bytes accessed | tf_op | source)
XLA Modules:
  0.0 118.4 jit_solution(4664373140665038669)
XLA Ops:
  0.0 0.0 copy-start
  0.0 1.4 %copy-done = bf16[1024,768]{1,0:T(8,128)(2,1)S(1)} copy-done((bf16[1024,768]{1,0:T(8,128)(2,1)S(1)}, bf16[1024,768]{1,0:T(8,128)(2,1)}, u32[]{:S(2)}) %copy-start) | copy-done | bytes 1572888
  1.4 0.0 copy-start.1
  1.4 1.2 %copy-done.1 = bf16[512,1024]{1,0:T(8,128)(2,1)S(1)} copy-done((bf16[512,1024]{1,0:T(8,128)(2,1)S(1)}, bf16[512,1024]{1,0:T(8,128)(2,1)}, u32[]{:S(2)}) %copy-start.1) | copy-done | bytes 1048600
  2.6 0.0 copy-start.2
  2.6 0.7 copy-done.2
  3.3 0.0 copy-start.4
  3.3 0.7 copy-done.4
  4.0 0.0 copy-start.5
  4.0 0.7 copy-done.5
  4.7 2.0 %project.1 = bf16[256,1664]{1,0:T(8,128)(2,1)S(1)} custom-call(bf16[512,1024]{1,0:T(8,128)(2,1)S(1)} %copy-done.1, bf16[1024,768]{1,0:T(8,128)(2,1)S(1)} %copy-done, s32[1,512]{1,0:T(1,128)S(1)} %bitcast.8, s32[1,512]{1,0:T(1,128)S(1)} %bitcast.9, s32[1,128]{1,0:T(1,128)S(1)} %bitcast.6), custom_call_target="tpu_custom_call" | custom-call | tf_op jit(solution)/shard_map/project/pallas_call | solution.py:101
  6.7 0.3 reshape.24
  7.0 71.4 %all_to_all.5 = bf16[128,2,1664]{2,1,0:T(2,128)(2,1)S(1)} all-to-all(bf16[128,2,1664]{2,1,0:T(2,128)(2,1)S(1)} %reshape.24), channel_id=1, replica_groups={{0,4,11,29,18,22,25,15,32,36,43,61,50,54,57,47,64,68,75,93,82,86,89,79,..., dimensions={0} | all-to-all | bytes 1703936 | tf_op jit(solution)/shard_map/all_to_all | solution.py:110
  78.4 0.0 copy-start.7
  78.4 0.6 fusion
  79.0 0.3 copy-done.7
  79.3 0.0 copy-start.3
  79.3 0.0 copy-start.6
  79.3 0.9 slice.13
  80.3 1.9 %collective-permute-start = (bf16[128,1664]{1,0:T(8,128)(2,1)}, bf16[128,1664]{1,0:T(8,128)(2,1)S(1)}, u32[]{:S(2)}, u32[]{:S(2)}) collective-permute-start(bf16[128,1664]{1,0:T(8,128)(2,1)} %slice.13), channel_id=1, source_target_pairs={{0,1},{1,2},{2,3},{3,0},{8,9},{9,10},{10,11},{11,8},{16,17},{17,18... | collective-permute-start | bytes 1277960 | tf_op jit(solution)/shard_map/ppermute | solution.py:99
  82.2 0.9 slice.15
  83.1 4.6 %collective-permute-start.1 = (bf16[128,1664]{1,0:T(8,128)(2,1)}, bf16[128,1664]{1,0:T(8,128)(2,1)S(1)}, u32[]{:S(2)}, u32[]{:S(2)}) collective-permute-start(bf16[128,1664]{1,0:T(8,128)(2,1)} %slice.15), channel_id=1, source_target_pairs={{0,3},{1,0},{2,1},{3,2},{8,11},{9,8},{10,9},{11,10},{16,19},{17,16... | collective-permute-start | bytes 1277960 | tf_op jit(solution)/shard_map/ppermute | solution.py:99
  87.7 1.9 %collective-permute-start.3 = (bf16[128,1664]{1,0:T(8,128)(2,1)}, bf16[128,1664]{1,0:T(8,128)(2,1)S(1)}, u32[]{:S(2)}, u32[]{:S(2)}) collective-permute-start(bf16[128,1664]{1,0:T(8,128)(2,1)} %slice.13), channel_id=1, source_target_pairs={{0,3},{1,0},{2,1},{3,2},{8,11},{9,8},{10,9},{11,10},{16,19},{17,16... | collective-permute-start | bytes 1277960 | tf_op jit(solution)/shard_map/ppermute | solution.py:99
  89.6 3.4 %collective-permute-start.2 = (bf16[128,1664]{1,0:T(8,128)(2,1)}, bf16[128,1664]{1,0:T(8,128)(2,1)S(1)}, u32[]{:S(2)}, u32[]{:S(2)}) collective-permute-start(bf16[128,1664]{1,0:T(8,128)(2,1)} %slice.15), channel_id=1, source_target_pairs={{0,1},{1,2},{2,3},{3,0},{8,9},{9,10},{10,11},{11,8},{16,17},{17,18... | collective-permute-start | bytes 1277960 | tf_op jit(solution)/shard_map/ppermute | solution.py:99
  93.0 0.0 collective-permute-done.refs_4_
  93.0 1.9 %collective-permute-start.4 = (bf16[128,1664]{1,0:T(8,128)(2,1)S(1)}, bf16[128,1664]{1,0:T(8,128)(2,1)S(1)}, u32[]{:S(2)}, u32[]{:S(2)}) collective-permute-start(bf16[128,1664]{1,0:T(8,128)(2,1)S(1)} %collective-permute-done.refs_4_), channel_id=1, source_target_pairs={{0,1},{1,2},{2,3},{3,0},{8,9},{9,10},{10,11},{11,8},{16,17},{17,18... | collective-permute-start | bytes 1277960 | tf_op jit(solution)/shard_map/ppermute | solution.py:99
  94.9 0.0 collective-permute-done.1.refs_5_
  94.9 4.6 %collective-permute-start.5 = (bf16[128,1664]{1,0:T(8,128)(2,1)S(1)}, bf16[128,1664]{1,0:T(8,128)(2,1)S(1)}, u32[]{:S(2)}, u32[]{:S(2)}) collective-permute-start(bf16[128,1664]{1,0:T(8,128)(2,1)S(1)} %collective-permute-done.1.refs_5_), channel_id=1, source_target_pairs={{0,3},{1,0},{2,1},{3,2},{8,11},{9,8},{10,9},{11,10},{16,19},{17,16... | collective-permute-start | bytes 1277960 | tf_op jit(solution)/shard_map/ppermute | solution.py:99
  99.5 0.1 pad_add_fusion.refs_0_
  99.6 2.4 %reshape.25.refs_3_ = bf16[256,1664]{1,0:T(8,128)(2,1)S(1)} reshape(bf16[128,2,1664]{2,1,0:T(2,128)(2,1)} %copy-done.7) | data formatting | bytes 1703936 | tf_op jit(solution)/shard_map/reshape | solution.py:112
  102.0 0.0 collective-permute-done.3.refs_7_
  102.0 0.0 collective-permute-done.2.refs_6_
  102.0 2.7 %collective-permute-done.4.refs_8_ = bf16[128,1664]{1,0:T(8,128)(2,1)S(1)} collective-permute-done((bf16[128,1664]{1,0:T(8,128)(2,1)S(1)}, bf16[128,1664]{1,0:T(8,128)(2,1)S(1)}, u32[]{:S(2)}, u32[]{:S(2)}) %collective-permute-start.4) | collective-permute-done | bytes 426016 | tf_op jit(solution)/shard_map/ppermute | solution.py:99
  104.7 0.0 collective-permute-done.5.refs_9_
  104.7 0.0 copy-done.3
  104.7 0.0 copy-done.6
  104.7 5.5 %gram.1 = f32[1,512]{1,0:T(1,128)S(1)} custom-call(s32[2]{0:T(128)S(1)} %pad_add_fusion.refs_0_, s32[1,128]{1,0:T(1,128)S(1)} %bitcast.7, s32[1,128]{1,0:T(1,128)S(1)} %bitcast.10, bf16[256,1664]{1,0:T(8,128)(2,1)S(1)} %reshape.25.refs_3_, bf16[128,1664]{1,0:T(8,128)(2,1)S(1)} %collective-permute-done.refs_4_, ...), custom_call_target="tpu_custom_call" | custom-call | tf_op jit(solution)/shard_map/gram/pallas_call | solution.py:123
  110.2 2.0 %collective-permute-start.6 = (f32[1,512]{1,0:T(1,128)S(1)}, f32[1,512]{1,0:T(1,128)S(1)}, u32[]{:S(2)}, u32[]{:S(2)}) collective-permute-start(f32[1,512]{1,0:T(1,128)S(1)} %gram.1), channel_id=1, source_target_pairs={{0,0},{1,1},{2,2},{3,3},{8,8},{9,9},{10,10},{11,11},{16,16},{17,17... | collective-permute-start | bytes 6152 | tf_op jit(solution)/shard_map/ppermute | solution.py:133
  112.2 5.6 %collective-permute-done.6 = f32[1,512]{1,0:T(1,128)S(1)} collective-permute-done((f32[1,512]{1,0:T(1,128)S(1)}, f32[1,512]{1,0:T(1,128)S(1)}, u32[]{:S(2)}, u32[]{:S(2)}) %collective-permute-start.6) | collective-permute-done | bytes 2080 | tf_op jit(solution)/shard_map/ppermute | solution.py:133
  117.9 0.6 copy.8
Async XLA Ops:
  0.0 1.4 %copy-start = (bf16[1024,768]{1,0:T(8,128)(2,1)S(1)}, bf16[1024,768]{1,0:T(8,128)(2,1)}, u32[]{:S(2)}) copy-start(bf16[1024,768]{1,0:T(8,128)(2,1)} %refs_1_.1) | copy-start | bytes 4718596
  1.4 1.2 %copy-start.1 = (bf16[512,1024]{1,0:T(8,128)(2,1)S(1)}, bf16[512,1024]{1,0:T(8,128)(2,1)}, u32[]{:S(2)}) copy-start(bf16[512,1024]{1,0:T(8,128)(2,1)} %refs_0_.1) | copy-start | bytes 3145732
  2.6 0.7 copy-start.2
  3.3 0.7 copy-start.4
  4.0 0.7 copy-start.5
  78.4 0.9 copy-start.7
  79.3 25.4 %copy-start.3 = (s32[128]{0:T(128)S(1)}, s32[128]{0:T(128)}, u32[]{:S(2)}) copy-start(s32[128]{0:T(128)} %param.10) | copy-start | bytes 1540
  79.3 25.4 %copy-start.6 = (s32[128]{0:T(128)S(1)}, s32[128]{0:T(128)}, u32[]{:S(2)}) copy-start(s32[128]{0:T(128)} %param.11) | copy-start | bytes 1540
  80.3 12.7 %collective-permute-start = (bf16[128,1664]{1,0:T(8,128)(2,1)}, bf16[128,1664]{1,0:T(8,128)(2,1)S(1)}, u32[]{:S(2)}, u32[]{:S(2)}) collective-permute-start(bf16[128,1664]{1,0:T(8,128)(2,1)} %slice.13), channel_id=1, source_target_pairs={{0,1},{1,2},{2,3},{3,0},{8,9},{9,10},{10,11},{11,8},{16,17},{17,18... | collective-permute-start | bytes 1277960 | tf_op jit(solution)/shard_map/ppermute | solution.py:99
  83.1 11.8 %collective-permute-start.1 = (bf16[128,1664]{1,0:T(8,128)(2,1)}, bf16[128,1664]{1,0:T(8,128)(2,1)S(1)}, u32[]{:S(2)}, u32[]{:S(2)}) collective-permute-start(bf16[128,1664]{1,0:T(8,128)(2,1)} %slice.15), channel_id=1, source_target_pairs={{0,3},{1,0},{2,1},{3,2},{8,11},{9,8},{10,9},{11,10},{16,19},{17,16... | collective-permute-start | bytes 1277960 | tf_op jit(solution)/shard_map/ppermute | solution.py:99
  87.7 14.3 %collective-permute-start.3 = (bf16[128,1664]{1,0:T(8,128)(2,1)}, bf16[128,1664]{1,0:T(8,128)(2,1)S(1)}, u32[]{:S(2)}, u32[]{:S(2)}) collective-permute-start(bf16[128,1664]{1,0:T(8,128)(2,1)} %slice.13), channel_id=1, source_target_pairs={{0,3},{1,0},{2,1},{3,2},{8,11},{9,8},{10,9},{11,10},{16,19},{17,16... | collective-permute-start | bytes 1277960 | tf_op jit(solution)/shard_map/ppermute | solution.py:99
  89.6 12.4 %collective-permute-start.2 = (bf16[128,1664]{1,0:T(8,128)(2,1)}, bf16[128,1664]{1,0:T(8,128)(2,1)S(1)}, u32[]{:S(2)}, u32[]{:S(2)}) collective-permute-start(bf16[128,1664]{1,0:T(8,128)(2,1)} %slice.15), channel_id=1, source_target_pairs={{0,1},{1,2},{2,3},{3,0},{8,9},{9,10},{10,11},{11,8},{16,17},{17,18... | collective-permute-start | bytes 1277960 | tf_op jit(solution)/shard_map/ppermute | solution.py:99
  93.0 11.8 %collective-permute-start.4 = (bf16[128,1664]{1,0:T(8,128)(2,1)S(1)}, bf16[128,1664]{1,0:T(8,128)(2,1)S(1)}, u32[]{:S(2)}, u32[]{:S(2)}) collective-permute-start(bf16[128,1664]{1,0:T(8,128)(2,1)S(1)} %collective-permute-done.refs_4_), channel_id=1, source_target_pairs={{0,1},{1,2},{2,3},{3,0},{8,9},{9,10},{10,11},{11,8},{16,17},{17,18... | collective-permute-start | bytes 1277960 | tf_op jit(solution)/shard_map/ppermute | solution.py:99
  94.9 9.8 %collective-permute-start.5 = (bf16[128,1664]{1,0:T(8,128)(2,1)S(1)}, bf16[128,1664]{1,0:T(8,128)(2,1)S(1)}, u32[]{:S(2)}, u32[]{:S(2)}) collective-permute-start(bf16[128,1664]{1,0:T(8,128)(2,1)S(1)} %collective-permute-done.1.refs_5_), channel_id=1, source_target_pairs={{0,3},{1,0},{2,1},{3,2},{8,11},{9,8},{10,9},{11,10},{16,19},{17,16... | collective-permute-start | bytes 1277960 | tf_op jit(solution)/shard_map/ppermute | solution.py:99
  110.2 7.6 %collective-permute-start.6 = (f32[1,512]{1,0:T(1,128)S(1)}, f32[1,512]{1,0:T(1,128)S(1)}, u32[]{:S(2)}, u32[]{:S(2)}) collective-permute-start(f32[1,512]{1,0:T(1,128)S(1)} %gram.1), channel_id=1, source_target_pairs={{0,0},{1,1},{2,2},{3,3},{8,8},{9,9},{10,10},{11,11},{16,16},{17,17... | collective-permute-start | bytes 6152 | tf_op jit(solution)/shard_map/ppermute | solution.py:133

commit v2 on v1

v2 whole, which is shorter than its diff:
```python
import jax
import jax.numpy as jnp
from jax import lax
from jax.experimental import pallas as pl
from jax.experimental.pallas import tpu as pltpu
from jax.sharding import PartitionSpec as P

TILE = 2048
EPS = 1e-06
AXES = ("dp", "split")
NT = (((1,), (1,)), ((), ()))
FAR = 1e9


def iota(shape, dim):
    return lax.broadcasted_iota(jnp.int32, shape, dim)


def bf16(mask_or_int):
    return mask_or_int.astype(jnp.float32).astype(jnp.bfloat16)


def project_kernel(
    splits, block, features_hbm, weight_hbm, cluster_hbm, rank_hbm, owner_hbm, out_ref,
    features, weight, cluster_ref, rank_ref, owner_ref, semaphores,
):
    half = features.shape[1] // 2
    copies = []
    for i in range(2):
        part = pl.ds(i * half, half)
        copies.append((weight_hbm.at[part, :], weight.at[part, :]))
        copies.append((features_hbm.at[:, part], features.at[:, part]))
    copies += [(cluster_hbm, cluster_ref), (rank_hbm, rank_ref), (owner_hbm, owner_ref)]
    copies = [pltpu.make_async_copy(*pair, semaphores.at[i]) for i, pair in enumerate(copies)]
    for copy in copies[4:] + copies[:4]:
        copy.start()
    for copy in copies[4:]:
        copy.wait()
    cluster, rank = cluster_ref[...], rank_ref[...]
    clusters, rows, width = owner_ref.shape[1], cluster.shape[1], weight.shape[1]
    owner = bf16(jnp.broadcast_to(owner_ref[...], (8, clusters)))
    named = bf16(iota((clusters, rows), 0) == cluster)
    slot = jnp.dot(owner, named, preferred_element_type=jnp.float32)[0:1].astype(jnp.int32)
    place = jnp.where(cluster >= 0, slot * splits + rank // block, -1)
    high, low = (rank + 1) // 16, (rank + 1) % 16
    lane = iota((128, rows), 0)
    numbers = jnp.zeros((rows // 2, 128), jnp.float32)
    chosen = [bf16(2 * iota((rows // 2, rows), 0) + i == place) for i in range(2)]
    for i in range(2):
        digits = bf16(jnp.where(lane == 2 * i, high, jnp.where(lane == 2 * i + 1, low, 0)))
        numbers += lax.dot_general(chosen[i], digits, NT, preferred_element_type=jnp.float32)
    out_ref[:, 2 * width :] = numbers.astype(jnp.bfloat16)

    copies[0].wait()
    copies[1].wait()
    projected = jnp.dot(features[:, :half], weight[:half, :], preferred_element_type=jnp.float32)
    copies[2].wait()
    copies[3].wait()
    projected += jnp.dot(features[:, half:], weight[half:, :], preferred_element_type=jnp.float32)
    normed = projected * lax.rsqrt(jnp.sum(projected * projected, axis=1, keepdims=True) + EPS)
    normed = normed.astype(jnp.bfloat16)
    for i in range(2):
        sent = jnp.dot(chosen[i], normed, preferred_element_type=jnp.float32)
        out_ref[:, i * width : (i + 1) * width] = sent.astype(jnp.bfloat16)


class Members:
    def __init__(self, ref, width, step):
        self.ref, self.width, self.step = ref, width, step

    def number(self, digits, first):
        weight = jnp.where(iota((128, self.step), 0) == first, 16, jnp.where(iota((128, self.step), 0) == first + 1, 1, 0))
        return jnp.dot(digits, bf16(weight), preferred_element_type=jnp.float32)

    def halves(self):
        digits = self.ref[:, 2 * self.width :]
        for i in range(2):
            number = self.number(digits, 2 * i)
            yield self.ref[:, i * self.width : (i + 1) * self.width], jnp.where(number > 0, number, FAR)

    def own(self, block_index):
        start = pl.multiple_of(block_index // 2 * self.step, self.step)
        column = pl.multiple_of(block_index % 2 * self.width, 128)
        rows = self.ref[pl.ds(start, self.step), pl.ds(column, self.width)]
        digits = self.ref[pl.ds(start, self.step), 2 * self.width :]
        first = 2 * (block_index % 2)
        weight = jnp.where(iota((8, 128), 1) == first, 16, jnp.where(iota((8, 128), 1) == first + 1, 1, 0))
        along = lax.dot_general(bf16(weight), digits, NT, preferred_element_type=jnp.float32)[0:1]
        return rows, along, self.number(digits, first)


def earlier_max(best, members, queries, numbers):
    step = numbers[0].shape[1]
    for part in members:
        for rows, number in part.halves():
            scores = lax.dot_general(rows, queries, NT, preferred_element_type=jnp.float32)
            for i, query_number in enumerate(numbers):
                found = jnp.where(number < query_number, scores[:, i * step : (i + 1) * step], -1.0)
                best[i] = jnp.maximum(best[i], jnp.max(found.reshape(-1, 8, step), axis=0))
    return best


def near_kernel(width, step, index_ref, own_ref, left_ref, right_ref, out_ref):
    parts = [Members(ref, width, step) for ref in (own_ref, left_ref, right_ref)]
    rows, numbers, _ = zip(*[part.own(index_ref[1]) for part in parts])
    best = [jnp.full((8, step), -1.0, jnp.float32) for _ in parts]
    best = earlier_max(best, parts, jnp.concatenate(rows, axis=0), numbers)
    for i, found in enumerate(best):
        out_ref[:, i * step : (i + 1) * step] = found


def far_kernel(width, step, index_ref, owner_ref, size_ref, own_ref, left_ref, right_ref, far_ref, near_ref, out_ref):
    block = out_ref.shape[1]
    parts = [Members(ref, width, step) for ref in (own_ref, left_ref, right_ref, far_ref)]
    rows, numbers, columns = zip(*[part.own(index_ref[1]) for part in parts])
    best = [near_ref[:, i * step : (i + 1) * step] for i in range(3)] + [jnp.full((8, step), -1.0, jnp.float32)]
    best[3:] = earlier_max(best[3:], parts[:3], rows[3], numbers[3:])
    best = earlier_max(best, parts[3:], jnp.concatenate(rows, axis=0), numbers)
    best = jnp.concatenate([jnp.max(found, axis=0, keepdims=True) for found in best], axis=1)

    start = index_ref[1] * block
    target = (start + 1 + iota((1, block), 1)).astype(jnp.float32)
    chosen = jnp.concatenate(
        [
            jnp.concatenate([bf16(column == target[:, i * step : (i + 1) * step]) for i in range(block // step)], axis=1)
            for column in columns
        ],
        axis=0,
    )
    first = best.astype(jnp.bfloat16)
    rest = best - first.astype(jnp.float32)
    second = rest.astype(jnp.bfloat16)
    third = (rest - second.astype(jnp.float32)).astype(jnp.bfloat16)
    line = iota((8, best.shape[1]), 0)
    terms = [jnp.broadcast_to(term.astype(jnp.float32), line.shape) for term in (first, second, third)]
    split = jnp.where(line == 0, terms[0], jnp.where(line == 1, terms[1], jnp.where(line == 2, terms[2], 0.0)))
    found = jnp.dot(split.astype(jnp.bfloat16), chosen, preferred_element_type=jnp.float32)
    ordered = found[0:1] + found[1:2] + found[2:3]
    size = jnp.sum(jnp.where(owner_ref[...] == index_ref[0], size_ref[...], 0), axis=1, keepdims=True)
    out_ref[...] = jnp.where(start + iota((1, block), 1) < size, ordered, -1.0)


def local(features, proj_weight, row_cluster, row_rank, owner_slot, tile_size):
    owners, splits = lax.axis_size("dp"), lax.axis_size("split")
    planes = owners // (2 * splits)
    rows, width = features.shape[0], proj_weight.shape[1]
    block = TILE // splits
    hbm = pl.BlockSpec(memory_space=pl.ANY)
    vmem = pl.BlockSpec(memory_space=pltpu.VMEM)
    smem = pl.BlockSpec(memory_space=pltpu.SMEM)
    params = pltpu.CompilerParams(vmem_limit_bytes=40 * 1024 * 1024)
    owner_row = owner_slot.reshape(1, -1)

    def device(z, y, core, x):
        return ((z * splits + y) * 2 + core) * splits + x

    everywhere = [(z, a, b) for z in range(planes) for a in range(splits) for b in range(splits)]
    diagonals = [
        [
            device(z, (g - j) % splits, 1, j) if core else device(z, j, 0, (g - j) % splits)
            for z in range(planes)
            for j in range(splits)
            for core in range(2)
        ]
        for g in range(splits)
    ]

    def shift(array, step):
        pairs = [(device(z, a, 0, b), device(z, a, 0, (b + step) % splits)) for z, a, b in everywhere]
        pairs += [(device(z, a, 1, b), device(z, (a + step) % splits, 1, b)) for z, a, b in everywhere]
        return lax.ppermute(array, AXES, pairs)

    outgoing = pl.pallas_call(
        lambda *refs: project_kernel(splits, block, *refs),
        out_shape=jax.ShapeDtypeStruct((rows // 2, 2 * width + 128), jnp.bfloat16),
        in_specs=[hbm] * 5,
        out_specs=vmem,
        scratch_shapes=[
            pltpu.VMEM(features.shape, jnp.bfloat16),
            pltpu.VMEM(proj_weight.shape, jnp.bfloat16),
            pltpu.VMEM((1, rows), jnp.int32),
            pltpu.VMEM((1, rows), jnp.int32),
            pltpu.VMEM(owner_row.shape, jnp.int32),
            pltpu.SemaphoreType.DMA((7,)),
        ],
        compiler_params=pltpu.CompilerParams(vmem_limit_bytes=60 * 1024 * 1024),
        name="project",
    )(features, proj_weight, row_cluster.reshape(1, rows), row_rank.reshape(1, rows), owner_row)

    own = lax.all_to_all(
        outgoing.reshape(owners, splits // 2, -1), AXES, 0, 0, tiled=True, axis_index_groups=diagonals
    )
    own = own.transpose(1, 0, 2).reshape(rows // 2, -1)
    left, right, far = shift(own, 1), shift(own, -1), shift(own, 2)

    owner, x = lax.axis_index("dp"), lax.axis_index("split")
    z, y, core = owner // (2 * splits), owner // 2 % splits, owner % 2
    index = jnp.stack(
        [jnp.where(core == 0, owner, (z * splits + x) * 2 + 1), jnp.where(core == 0, x, y)]
    ).astype(jnp.int32)
    near_best = pl.pallas_call(
        lambda *refs: near_kernel(width, owners, *refs),
        out_shape=jax.ShapeDtypeStruct((8, 3 * owners), jnp.float32),
        in_specs=[smem] + [vmem] * 3,
        out_specs=vmem,
        compiler_params=params,
        name="near",
        cost_estimate=pl.CostEstimate(flops=2 * 3 * owners * 3 * rows * width, bytes_accessed=3 << 20, transcendentals=0),
    )(index, own, left, right)
    best = pl.pallas_call(
        lambda *refs: far_kernel(width, owners, *refs),
        out_shape=jax.ShapeDtypeStruct((1, block), jnp.float32),
        in_specs=[smem] + [vmem] * 7,
        out_specs=vmem,
        compiler_params=params,
        name="far",
    )(index, owner_row, tile_size.reshape(1, -1), own, left, right, far, near_best)
    home = [(device(z, a, 0, b), device(z, a, 0, b)) for z, a, b in everywhere]
    home += [(device(z, a, 1, b), device(z, b, 1, a)) for z, a, b in everywhere]
    return lax.ppermute(best, AXES, home)


def solution(mesh):
    return jax.shard_map(
        local,
        mesh=mesh,
        in_specs=(P(("dp", "split"), None), P(), P(("dp", "split")), P(("dp", "split")), P(), P()),
        out_specs=P("dp", "split"),
        check_vma=False,
    )
```

time: 119 us -> 118 us (level)
  the two profiles are of different devices: /device:TPU:7 before, /device:TPU:5 now
where the time goes in v2:
time: 118 us; the launch traced here: 117 us
  blocking collectives  68.1 us (58%)
  waiting for transfers between devices  24.9 us (21%)
  starting transfers between devices  12.4 us (11%)
  Pallas kernels  8.9 us (8%)
  local copies, waits for them, and re-layouts  2.92 us (2%)
    all_to_all x1, blocking collectives, local(): lax.all_to_all(outgoing.reshape(owners, splits // 2, -1), AXES, 0, 0, til...  68.1 us
    ppermute x3, waiting for transfers between devices, shift(): return lax.ppermute(array, AXES, pairs)  18.6 us
    ppermute x3, starting transfers between devices, shift(): return lax.ppermute(array, AXES, pairs)  10.5 us
    ppermute x1, waiting for transfers between devices, local(): return lax.ppermute(best, AXES, home)  6.31 us
    pallas_call x1, Pallas kernels, local(): pl.pallas_call(lambda *refs: project_kernel(splits, block, *refs), out_sh...  4.64 us
  transfers between devices with their start and end apart: 4, of which 3 were waited for; matrix products, arithmetic and copies ran while one was open for 0% of the time, Pallas kernels for 2%

profile of v2, /device:TPU:5, one launch (start us, length us, event | category | flops | bytes accessed | tf_op | source)
XLA Modules:
  0.0 117.5 jit_solution(6873750541382200281)
XLA Ops:
  0.0 4.6 %project.1 = bf16[256,1664]{1,0:T(8,128)(2,1)} custom-call(bf16[512,1024]{1,0:T(8,128)(2,1)} %refs_0_.1, bf16[1024,768]{1,0:T(8,128)(2,1)} %refs_1_.1, s32[1,512]{1,0:T(1,128)} %bitcast.17, s32[1,512]{1,0:T(1,128)} %bitcast.18, s32[1,128]{1,0:T(1,128)} %bitcast.13), custom_call_target="tpu_custom_call" | custom-call | tf_op jit(solution)/shard_map/project/pallas_call | solution.py:173
  4.6 2.2 %reshape.22 = bf16[128,2,1664]{2,1,0:T(2,128)(2,1)S(1)} reshape(bf16[256,1664]{1,0:T(8,128)(2,1)} %project.1) | data formatting | bytes 1703936 | tf_op jit(solution)/shard_map/reshape | solution.py:191
  6.9 68.1 %all_to_all.5 = bf16[128,2,1664]{2,1,0:T(2,128)(2,1)S(1)} all-to-all(bf16[128,2,1664]{2,1,0:T(2,128)(2,1)S(1)} %reshape.22), channel_id=1, replica_groups={{0,4,11,29,18,22,25,15,32,36,43,61,50,54,57,47,64,68,75,93,82,86,89,79,..., dimensions={0} | all-to-all | bytes 1703936 | tf_op jit(solution)/shard_map/all_to_all | solution.py:190
  75.0 0.1 copy.8
  75.1 5.5 %collective-permute-start.1 = (bf16[256,1664]{1,0:T(8,128)(2,1)S(1)}, bf16[256,1664]{1,0:T(8,128)(2,1)S(1)}, u32[]{:S(2)}, u32[]{:S(2)}) collective-permute-start(bf16[256,1664]{1,0:T(8,128)(2,1)S(1)} %bitcast.8), channel_id=1, source_target_pairs={{0,3},{1,0},{2,1},{3,2},{8,11},{9,8},{10,9},{11,10},{16,19},{17,16... | collective-permute-start | bytes 2555912 | tf_op jit(solution)/shard_map/ppermute | solution.py:171
  80.6 1.9 %collective-permute-start = (bf16[256,1664]{1,0:T(8,128)(2,1)S(1)}, bf16[256,1664]{1,0:T(8,128)(2,1)S(1)}, u32[]{:S(2)}, u32[]{:S(2)}) collective-permute-start(bf16[256,1664]{1,0:T(8,128)(2,1)S(1)} %bitcast.9), channel_id=1, source_target_pairs={{0,1},{1,2},{2,3},{3,0},{8,9},{9,10},{10,11},{11,8},{16,17},{17,18... | collective-permute-start | bytes 2555912 | tf_op jit(solution)/shard_map/ppermute | solution.py:171
  82.5 3.1 %collective-permute-start.2 = (bf16[256,1664]{1,0:T(8,128)(2,1)S(1)}, bf16[256,1664]{1,0:T(8,128)(2,1)S(1)}, u32[]{:S(2)}, u32[]{:S(2)}) collective-permute-start(bf16[256,1664]{1,0:T(8,128)(2,1)S(1)} %bitcast.10), channel_id=1, source_target_pairs={{0,2},{1,3},{2,0},{3,1},{8,10},{9,11},{10,8},{11,9},{16,18},{17,19... | collective-permute-start | bytes 2555912 | tf_op jit(solution)/shard_map/ppermute | solution.py:171
  85.6 0.1 pad_add_fusion.refs_0_
  85.7 0.0 copy-start
  85.7 0.0 copy-start.1
  85.7 13.6 %collective-permute-done.1.refs_3_.refs_5_ = bf16[256,1664]{1,0:T(8,128)(2,1)S(1)} collective-permute-done((bf16[256,1664]{1,0:T(8,128)(2,1)S(1)}, bf16[256,1664]{1,0:T(8,128)(2,1)S(1)}, u32[]{:S(2)}, u32[]{:S(2)}) %collective-permute-start.1) | collective-permute-done | bytes 852000 | tf_op jit(solution)/shard_map/ppermute | solution.py:171
  99.3 5.0 %collective-permute-done.refs_2_.refs_4_ = bf16[256,1664]{1,0:T(8,128)(2,1)S(1)} collective-permute-done((bf16[256,1664]{1,0:T(8,128)(2,1)S(1)}, bf16[256,1664]{1,0:T(8,128)(2,1)S(1)}, u32[]{:S(2)}, u32[]{:S(2)}) %collective-permute-start) | collective-permute-done | bytes 852000 | tf_op jit(solution)/shard_map/ppermute | solution.py:171
  104.3 2.1 %near.1.refs_7_ = f32[8,384]{1,0:T(8,128)S(1)} custom-call(s32[2]{0:T(128)S(1)} %pad_add_fusion.refs_0_, bf16[256,1664]{1,0:T(8,128)(2,1)S(1)} %bitcast.11, bf16[256,1664]{1,0:T(8,128)(2,1)S(1)} %collective-permute-done.refs_2_.refs_4_, bf16[256,1664]{1,0:T(8,128)(2,1)S(1)} %collective-permute-done.1.refs_3_.refs_5_), custom_call_target="tpu_custom_call" | custom-call | flops 905969664 | bytes 3145728 | tf_op jit(solution)/shard_map/near/pallas_call | solution.py:201
  106.4 0.0 collective-permute-done.2.refs_6_
  106.5 0.0 copy-done
  106.5 0.0 copy-done.1
  106.5 2.2 %far.1 = f32[1,512]{1,0:T(1,128)S(1)} custom-call(s32[2]{0:T(128)S(1)} %pad_add_fusion.refs_0_, s32[1,128]{1,0:T(1,128)S(1)} %bitcast.14, s32[1,128]{1,0:T(1,128)S(1)} %bitcast.15, bf16[256,1664]{1,0:T(8,128)(2,1)S(1)} %bitcast.12, bf16[256,1664]{1,0:T(8,128)(2,1)S(1)} %collective-permute-done.refs_2_.refs_4_, ...), custom_call_target="tpu_custom_call" | custom-call | tf_op jit(solution)/shard_map/far/pallas_call | solution.py:210
  108.6 1.9 %collective-permute-start.3 = (f32[1,512]{1,0:T(1,128)S(1)}, f32[1,512]{1,0:T(1,128)S(1)}, u32[]{:S(2)}, u32[]{:S(2)}) collective-permute-start(f32[1,512]{1,0:T(1,128)S(1)} %far.1), channel_id=1, source_target_pairs={{0,0},{1,1},{2,2},{3,3},{8,8},{9,9},{10,10},{11,11},{16,16},{17,17... | collective-permute-start | bytes 6152 | tf_op jit(solution)/shard_map/ppermute | solution.py:220
  110.6 6.3 %collective-permute-done.3 = f32[1,512]{1,0:T(1,128)S(1)} collective-permute-done((f32[1,512]{1,0:T(1,128)S(1)}, f32[1,512]{1,0:T(1,128)S(1)}, u32[]{:S(2)}, u32[]{:S(2)}) %collective-permute-start.3) | collective-permute-done | bytes 2080 | tf_op jit(solution)/shard_map/ppermute | solution.py:220
  116.9 0.6 copy.10
Async XLA Ops:
  75.1 24.2 %collective-permute-start.1 = (bf16[256,1664]{1,0:T(8,128)(2,1)S(1)}, bf16[256,1664]{1,0:T(8,128)(2,1)S(1)}, u32[]{:S(2)}, u32[]{:S(2)}) collective-permute-start(bf16[256,1664]{1,0:T(8,128)(2,1)S(1)} %bitcast.8), channel_id=1, source_target_pairs={{0,3},{1,0},{2,1},{3,2},{8,11},{9,8},{10,9},{11,10},{16,19},{17,16... | collective-permute-start | bytes 2555912 | tf_op jit(solution)/shard_map/ppermute | solution.py:171
  80.6 23.8 %collective-permute-start = (bf16[256,1664]{1,0:T(8,128)(2,1)S(1)}, bf16[256,1664]{1,0:T(8,128)(2,1)S(1)}, u32[]{:S(2)}, u32[]{:S(2)}) collective-permute-start(bf16[256,1664]{1,0:T(8,128)(2,1)S(1)} %bitcast.9), channel_id=1, source_target_pairs={{0,1},{1,2},{2,3},{3,0},{8,9},{9,10},{10,11},{11,8},{16,17},{17,18... | collective-permute-start | bytes 2555912 | tf_op jit(solution)/shard_map/ppermute | solution.py:171
  82.5 24.0 %collective-permute-start.2 = (bf16[256,1664]{1,0:T(8,128)(2,1)S(1)}, bf16[256,1664]{1,0:T(8,128)(2,1)S(1)}, u32[]{:S(2)}, u32[]{:S(2)}) collective-permute-start(bf16[256,1664]{1,0:T(8,128)(2,1)S(1)} %bitcast.10), channel_id=1, source_target_pairs={{0,2},{1,3},{2,0},{3,1},{8,10},{9,11},{10,8},{11,9},{16,18},{17,19... | collective-permute-start | bytes 2555912 | tf_op jit(solution)/shard_map/ppermute | solution.py:171
  85.7 20.7 %copy-start = (s32[128]{0:T(128)S(1)}, s32[128]{0:T(128)}, u32[]{:S(2)}) copy-start(s32[128]{0:T(128)} %param.10) | copy-start | bytes 1540
  85.7 20.8 %copy-start.1 = (s32[128]{0:T(128)S(1)}, s32[128]{0:T(128)}, u32[]{:S(2)}) copy-start(s32[128]{0:T(128)} %param.11) | copy-start | bytes 1540
  108.6 8.2 %collective-permute-start.3 = (f32[1,512]{1,0:T(1,128)S(1)}, f32[1,512]{1,0:T(1,128)S(1)}, u32[]{:S(2)}, u32[]{:S(2)}) collective-permute-start(f32[1,512]{1,0:T(1,128)S(1)} %far.1), channel_id=1, source_target_pairs={{0,0},{1,1},{2,2},{3,3},{8,8},{9,9},{10,10},{11,11},{16,16},{17,17... | collective-permute-start | bytes 6152 | tf_op jit(solution)/shard_map/ppermute | solution.py:220

commit v3 on v1

v3 whole, which is shorter than its diff:
```python
import jax
import jax.numpy as jnp
from jax import lax
from jax.experimental import pallas as pl
from jax.experimental.pallas import tpu as pltpu
from jax.sharding import PartitionSpec as P

TILE = 2048
EPS = 1e-06
NT = (((1,), (1,)), ((), ()))
FAR = 1e9


def iota(shape, dim):
    return lax.broadcasted_iota(jnp.int32, shape, dim)


def bf16(mask_or_int):
    return mask_or_int.astype(jnp.float32).astype(jnp.bfloat16)


def project_kernel(
    splits, block, features_hbm, weight_hbm, member_ref, owner_ref, out_ref, features, weight, semaphores,
):
    steps = 4
    part = features.shape[1] // steps
    pairs = []
    for i in range(steps):
        span = pl.ds(i * part, part)
        pairs.append((weight_hbm.at[span, :], weight.at[span, :]))
        pairs.append((features_hbm.at[:, span], features.at[:, span]))
    copies = [pltpu.make_async_copy(*pair, semaphores.at[i]) for i, pair in enumerate(pairs)]
    for copy in copies:
        copy.start()
    member = member_ref[...]
    clusters, rows, width = owner_ref.shape[1], member.shape[1], weight.shape[1]
    cluster, rank = member // TILE, member % TILE
    owner = bf16(jnp.broadcast_to(owner_ref[...], (8, clusters)))
    named = bf16(iota((clusters, rows), 0) == cluster)
    slot = jnp.dot(owner, named, preferred_element_type=jnp.float32)[0:1].astype(jnp.int32)
    place = jnp.where(member >= 0, slot * splits + rank // block, -1)
    high, low = (rank + 1) // 16, (rank + 1) % 16
    lane = iota((128, rows), 0)
    numbers = jnp.zeros((rows // 2, 128), jnp.float32)
    chosen = [bf16(2 * iota((rows // 2, rows), 0) + i == place) for i in range(2)]
    for i in range(2):
        digits = bf16(jnp.where(lane == 2 * i, high, jnp.where(lane == 2 * i + 1, low, 0)))
        numbers += lax.dot_general(chosen[i], digits, NT, preferred_element_type=jnp.float32)
    out_ref[:, 2 * width :] = numbers.astype(jnp.bfloat16)

    projected = jnp.zeros((rows, width), jnp.float32)
    for i in range(0, steps, 2):
        for copy in copies[2 * i : 4 + 2 * i]:
            copy.wait()
        span = slice(i * part, (i + 2) * part)
        projected += jnp.dot(features[:, span], weight[span, :], preferred_element_type=jnp.float32)
    normed = projected * lax.rsqrt(jnp.sum(projected * projected, axis=1, keepdims=True) + EPS)
    normed = normed.astype(jnp.bfloat16)
    for i in range(2):
        sent = jnp.dot(chosen[i], normed, preferred_element_type=jnp.float32)
        out_ref[:, i * width : (i + 1) * width] = sent.astype(jnp.bfloat16)


class Members:
    def __init__(self, ref, width, step):
        self.ref, self.width, self.step = ref, width, step

    def rows(self, index):
        span = slice(index // 2 * self.step, (index // 2 + 1) * self.step)
        return self.ref[span, index % 2 * self.width : (index % 2 + 1) * self.width]

    def weights(self, index, shape, dim):
        first = 2 * (index % 2)
        return bf16(jnp.where(iota(shape, dim) == first, 16, jnp.where(iota(shape, dim) == first + 1, 1, 0)))

    def digits(self, index):
        return self.ref[index // 2 * self.step : (index // 2 + 1) * self.step, 2 * self.width :]

    def down(self, index):
        weights = self.weights(index, (128, self.step), 0)
        return jnp.dot(self.digits(index), weights, preferred_element_type=jnp.float32)

    def along(self, index):
        weights = self.weights(index, (8, 128), 1)
        return lax.dot_general(weights, self.digits(index), NT, preferred_element_type=jnp.float32)[0:1]


def earlier_max(best, members, queries, numbers):
    splits, step = len(best), numbers[0].shape[1]
    for b in range(splits):
        rows = jnp.concatenate([part.rows(b) for part in members], axis=0)
        number = jnp.concatenate([part.down(b) for part in members], axis=0)
        number = jnp.where(number > 0, number, FAR)
        later = jnp.concatenate([queries.rows(a) for a in range(b, splits)], axis=0)
        scores = lax.dot_general(rows, later, NT, preferred_element_type=jnp.float32)
        for a in range(b, splits):
            found = jnp.where(number < numbers[a], scores[:, (a - b) * step : (a - b + 1) * step], -1.0)
            best[a] = jnp.maximum(best[a], jnp.max(found.reshape(-1, 8, step), axis=0))
    return best


def own_kernel(splits, width, step, own_ref, out_ref):
    own = Members(own_ref, width, step)
    best = [jnp.full((8, step), -1.0, jnp.float32) for _ in range(splits)]
    best = earlier_max(best, [own], own, [own.along(a) for a in range(splits)])
    for a in range(splits):
        out_ref[:, a * step : (a + 1) * step] = best[a]


def ring_kernel(splits, width, step, owner_index_ref, owner_ref, size_ref, own_ref, left_ref, right_ref, best_ref, out_ref):
    block = out_ref.shape[2]
    own, left, right = [Members(ref, width, step) for ref in (own_ref, left_ref, right_ref)]
    own_best = [best_ref[:, a * step : (a + 1) * step] for a in range(splits)]
    own_best = earlier_max(own_best, [left, right], own, [own.along(a) for a in range(splits)])
    left_best = [jnp.full((8, step), -1.0, jnp.float32) for _ in range(splits)]
    left_best = earlier_max(left_best, [right], left, [left.along(a) for a in range(splits)])

    size = jnp.sum(jnp.where(owner_ref[...] == owner_index_ref[0], size_ref[...], 0), axis=1, keepdims=True)
    for a in range(splits):
        rank = a * block + iota((1, block), 1)
        target = (rank + 1).astype(jnp.float32)
        column = jnp.concatenate([own.down(a), left.down(a)], axis=0)
        chosen = jnp.concatenate(
            [bf16(column == target[:, i * step : (i + 1) * step]) for i in range(block // step)], axis=1
        )
        best = jnp.concatenate(
            [jnp.max(own_best[a], axis=0, keepdims=True), jnp.max(left_best[a], axis=0, keepdims=True)], axis=1
        )
        first = best.astype(jnp.bfloat16)
        rest = best - first.astype(jnp.float32)
        second = rest.astype(jnp.bfloat16)
        third = (rest - second.astype(jnp.float32)).astype(jnp.bfloat16)
        line = iota((8, best.shape[1]), 0)
        terms = jnp.ones(line.shape, jnp.float32)
        for i, term in enumerate((first, second, third)):
            terms = jnp.where(line == i, term.astype(jnp.float32), terms)
        found = jnp.dot(terms.astype(jnp.bfloat16), chosen, preferred_element_type=jnp.float32)
        ordered = found[0:1] + found[1:2] + found[2:3]
        out_ref[a] = jnp.where((found[3:4] > 0) & (rank < size), ordered, -1.0)


def local(features, proj_weight, row_cluster, row_rank, owner_slot, tile_size):
    owners, splits = lax.axis_size("dp"), lax.axis_size("split")
    rows, width = features.shape[0], proj_weight.shape[1]
    block = TILE // splits
    hbm = pl.BlockSpec(memory_space=pltpu.HBM)
    vmem = pl.BlockSpec(memory_space=pltpu.VMEM)
    smem = pl.BlockSpec(memory_space=pltpu.SMEM)
    params = pltpu.CompilerParams(vmem_limit_bytes=32 * 1024 * 1024)
    owner_row = owner_slot.reshape(1, -1)
    member = jnp.where(row_cluster >= 0, row_cluster * TILE + row_rank, -1)

    outgoing = pl.pallas_call(
        lambda *refs: project_kernel(splits, block, *refs),
        out_shape=jax.ShapeDtypeStruct((rows // 2, 2 * width + 128), jnp.bfloat16),
        in_specs=[hbm] * 2 + [vmem] * 2,
        out_specs=vmem,
        scratch_shapes=[
            pltpu.VMEM(features.shape, jnp.bfloat16),
            pltpu.VMEM(proj_weight.shape, jnp.bfloat16),
            pltpu.SemaphoreType.DMA((8,)),
        ],
        compiler_params=pltpu.CompilerParams(vmem_limit_bytes=55200000),
        name="project",
    )(features, proj_weight, member.reshape(1, rows), owner_row)

    own = lax.all_to_all(outgoing.reshape(owners, splits // 2, -1), "dp", 0, 0, tiled=True)
    own = own.transpose(1, 0, 2).reshape(rows // 2, -1)
    left = lax.ppermute(own, "split", [(i, (i + 1) % splits) for i in range(splits)])
    right = lax.ppermute(own, "split", [(i, (i - 1) % splits) for i in range(splits)])

    best = pl.pallas_call(
        lambda *refs: own_kernel(splits, width, owners, *refs),
        out_shape=jax.ShapeDtypeStruct((8, splits * owners), jnp.float32),
        in_specs=[vmem],
        out_specs=vmem,
        compiler_params=params,
        name="own",
        cost_estimate=pl.CostEstimate(flops=2 * rows * rows * width, bytes_accessed=2 << 20, transcendentals=0),
    )(own)
    best = pl.pallas_call(
        lambda *refs: ring_kernel(splits, width, owners, *refs),
        out_shape=jax.ShapeDtypeStruct((splits, 1, block), jnp.float32),
        in_specs=[smem] + [vmem] * 6,
        out_specs=vmem,
        compiler_params=params,
        name="ring",
    )(lax.axis_index("dp").reshape(1), owner_row, tile_size.reshape(1, -1), own, left, right, best)
    return jnp.max(lax.all_to_all(best, "split", 0, 0, tiled=True), axis=0)


def solution(mesh):
    return jax.shard_map(
        local,
        mesh=mesh,
        in_specs=(P(("dp", "split"), None), P(), P(("dp", "split")), P(("dp", "split")), P(), P()),
        out_specs=P("dp", "split"),
        check_vma=False,
    )
```

time: 119 us -> 110 us (0.924)
  the two profiles are of different devices: /device:TPU:7 before, /device:TPU:32 now
where the time goes in v3:
time: 110 us
  blocking collectives  75.3 us (68%)
  waiting for transfers between devices  18.4 us (17%)
  starting transfers between devices  7.05 us (6%)
  Pallas kernels  6.84 us (6%)
  other arithmetic  1.3 us (1%)
    all_to_all x1, blocking collectives, local(): lax.all_to_all(outgoing.reshape(owners, splits // 2, -1), 'dp', 0, 0, til...  66 us
    ppermute x1, waiting for transfers between devices, local(): lax.ppermute(own, 'split', [(i, (i + 1) % splits) for i in range(splits)])  16.5 us
    all_to_all x1, blocking collectives, local(): return jnp.max(lax.all_to_all(best, 'split', 0, 0, tiled=True), axis=0)  9.35 us
    pallas_call x1, Pallas kernels, local(): pl.pallas_call(lambda *refs: project_kernel(splits, block, *refs), out_sh...  3.7 us
    ppermute x1, starting transfers between devices, local(): lax.ppermute(own, 'split', [(i, (i - 1) % splits) for i in range(splits)])  3.66 us
    ppermute x1, starting transfers between devices, local(): lax.ppermute(own, 'split', [(i, (i + 1) % splits) for i in range(splits)])  3.4 us
    pallas_call x1, Pallas kernels, local(): pl.pallas_call(lambda *refs: ring_kernel(splits, width, owners, *refs), o...  2.27 us
  transfers between devices with their start and end apart: 2, of which 2 were waited for; matrix products, arithmetic and copies ran while one was open for 0% of the time, Pallas kernels for 1%

profile of v3, /device:TPU:32, one launch (start us, length us, event | category | flops | bytes accessed | tf_op | source)
XLA Modules:
  0.0 110.1 jit_solution(2271979107731542178)
XLA Ops:
  0.0 0.7 add_select_fusion
  0.7 0.0 copy-start
  0.7 0.7 copy-done
  1.4 3.7 %project.1 = bf16[256,1664]{1,0:T(8,128)(2,1)S(1)} custom-call(bf16[512,1024]{1,0:T(8,128)(2,1)} %refs_0_.1, bf16[1024,768]{1,0:T(8,128)(2,1)} %refs_1_.1, s32[1,512]{1,0:T(1,128)S(1)} %bitcast.11, s32[1,128]{1,0:T(1,128)S(1)} %bitcast.12), custom_call_target="tpu_custom_call" | custom-call | tf_op jit(solution)/shard_map/project/pallas_call | solution.py:153
  5.1 0.3 reshape.23
  5.4 66.0 %all_to_all.10 = bf16[128,2,1664]{2,1,0:T(2,128)(2,1)S(1)} all-to-all(bf16[128,2,1664]{2,1,0:T(2,128)(2,1)S(1)} %reshape.23), channel_id=1, replica_groups=mesh['dp'=128,'split'=4] {'dp'}, dimensions={0} | all-to-all | bytes 1703936 | tf_op jit(solution)/shard_map/all_to_all | solution.py:167
  71.4 0.0 copy-start.1
  71.4 0.0 copy-start.2
  71.4 0.1 copy.8
  71.4 3.4 %collective-permute-start = (bf16[256,1664]{1,0:T(8,128)(2,1)S(1)}, bf16[256,1664]{1,0:T(8,128)(2,1)S(1)}, u32[]{:S(2)}, u32[]{:S(2)}) collective-permute-start(bf16[256,1664]{1,0:T(8,128)(2,1)S(1)} %bitcast.7), channel_id=1, source_target_pairs={{0,1},{1,2},{2,3},{3,0},{4,5},{5,6},{6,7},{7,4},{8,9},{9,10},{10,1... | collective-permute-start | bytes 2555912 | tf_op jit(solution)/shard_map/ppermute | solution.py:169
  74.9 3.7 %collective-permute-start.1 = (bf16[256,1664]{1,0:T(8,128)(2,1)S(1)}, bf16[256,1664]{1,0:T(8,128)(2,1)S(1)}, u32[]{:S(2)}, u32[]{:S(2)}) collective-permute-start(bf16[256,1664]{1,0:T(8,128)(2,1)S(1)} %bitcast.8), channel_id=1, source_target_pairs={{0,3},{1,0},{2,1},{3,2},{4,7},{5,4},{6,5},{7,6},{8,11},{9,8},{10,9... | collective-permute-start | bytes 2555912 | tf_op jit(solution)/shard_map/ppermute | solution.py:170
  78.5 0.9 own.1.refs_6_
  79.4 16.5 %collective-permute-done.refs_4_ = bf16[256,1664]{1,0:T(8,128)(2,1)S(1)} collective-permute-done((bf16[256,1664]{1,0:T(8,128)(2,1)S(1)}, bf16[256,1664]{1,0:T(8,128)(2,1)S(1)}, u32[]{:S(2)}, u32[]{:S(2)}) %collective-permute-start) | collective-permute-done | bytes 852000 | tf_op jit(solution)/shard_map/ppermute | solution.py:169
  95.9 1.9 %collective-permute-done.1.refs_5_ = bf16[256,1664]{1,0:T(8,128)(2,1)S(1)} collective-permute-done((bf16[256,1664]{1,0:T(8,128)(2,1)S(1)}, bf16[256,1664]{1,0:T(8,128)(2,1)S(1)}, u32[]{:S(2)}, u32[]{:S(2)}) %collective-permute-start.1) | collective-permute-done | bytes 852000 | tf_op jit(solution)/shard_map/ppermute | solution.py:170
  97.8 0.0 copy-done.1
  97.8 0.0 copy-done.2
  97.8 2.3 %ring.1 = f32[4,1,512]{2,1,0:T(1,128)S(1)} custom-call(s32[1]{0:T(128)} %bitcast.refs_0_, s32[1,128]{1,0:T(1,128)S(1)} %bitcast.13, s32[1,128]{1,0:T(1,128)S(1)} %bitcast.14, bf16[256,1664]{1,0:T(8,128)(2,1)S(1)} %bitcast.10, bf16[256,1664]{1,0:T(8,128)(2,1)S(1)} %collective-permute-done.refs_4_, bf16[256,1664]{1,0:T(8,128)(2,1)S(1)} %collective-permute-done.1.refs_5_, ...), custom_call_target="tpu_custom_call" | custom-call | tf_op jit(solution)/shard_map/ring/pallas_call | solution.py:181
  100.1 9.3 %all_to_all.11 = f32[4,1,512]{2,1,0:T(1,128)S(1)} all-to-all(f32[4,1,512]{2,1,0:T(1,128)S(1)} %ring.1), channel_id=1, replica_groups=mesh['dp'=128,'split'=4] {'split'}, dimensions={0} | all-to-all | bytes 16384 | tf_op jit(solution)/shard_map/all_to_all | solution.py:189
  109.5 0.6 reduce_max.11
Async XLA Ops:
  0.7 0.7 copy-start
  71.4 26.5 %copy-start.1 = (s32[128]{0:T(128)S(1)}, s32[128]{0:T(128)}, u32[]{:S(2)}) copy-start(s32[128]{0:T(128)} %param.10) | copy-start | bytes 1540
  71.4 26.5 %copy-start.2 = (s32[128]{0:T(128)S(1)}, s32[128]{0:T(128)}, u32[]{:S(2)}) copy-start(s32[128]{0:T(128)} %param.11) | copy-start | bytes 1540
  71.4 24.5 %collective-permute-start = (bf16[256,1664]{1,0:T(8,128)(2,1)S(1)}, bf16[256,1664]{1,0:T(8,128)(2,1)S(1)}, u32[]{:S(2)}, u32[]{:S(2)}) collective-permute-start(bf16[256,1664]{1,0:T(8,128)(2,1)S(1)} %bitcast.7), channel_id=1, source_target_pairs={{0,1},{1,2},{2,3},{3,0},{4,5},{5,6},{6,7},{7,4},{8,9},{9,10},{10,1... | collective-permute-start | bytes 2555912 | tf_op jit(solution)/shard_map/ppermute | solution.py:169
  74.9 23.0 %collective-permute-start.1 = (bf16[256,1664]{1,0:T(8,128)(2,1)S(1)}, bf16[256,1664]{1,0:T(8,128)(2,1)S(1)}, u32[]{:S(2)}, u32[]{:S(2)}) collective-permute-start(bf16[256,1664]{1,0:T(8,128)(2,1)S(1)} %bitcast.8), channel_id=1, source_target_pairs={{0,3},{1,0},{2,1},{3,2},{4,7},{5,4},{6,5},{7,6},{8,11},{9,8},{10,9... | collective-permute-start | bytes 2555912 | tf_op jit(solution)/shard_map/ppermute | solution.py:170

commit v4 on v3

--- a/solution.py
+++ b/solution.py
@@ -7,6 +7,7 @@
 
 TILE = 2048
 EPS = 1e-06
+AXES = ("dp", "split")
 NT = (((1,), (1,)), ((), ()))
 FAR = 1e9
 
@@ -107,7 +108,7 @@
         out_ref[:, a * step : (a + 1) * step] = best[a]
 
 
-def ring_kernel(splits, width, step, owner_index_ref, owner_ref, size_ref, own_ref, left_ref, right_ref, best_ref, out_ref):
+def ring_kernel(splits, width, step, index_ref, owner_ref, size_ref, own_ref, left_ref, right_ref, best_ref, out_ref):
     block = out_ref.shape[2]
     own, left, right = [Members(ref, width, step) for ref in (own_ref, left_ref, right_ref)]
     own_best = [best_ref[:, a * step : (a + 1) * step] for a in range(splits)]
@@ -115,7 +116,7 @@
     left_best = [jnp.full((8, step), -1.0, jnp.float32) for _ in range(splits)]
     left_best = earlier_max(left_best, [right], left, [left.along(a) for a in range(splits)])
 
-    size = jnp.sum(jnp.where(owner_ref[...] == owner_index_ref[0], size_ref[...], 0), axis=1, keepdims=True)
+    size = jnp.sum(jnp.where(owner_ref[...] == index_ref[0], size_ref[...], 0), axis=1, keepdims=True)
     for a in range(splits):
         rank = a * block + iota((1, block), 1)
         target = (rank + 1).astype(jnp.float32)
@@ -136,11 +137,14 @@
             terms = jnp.where(line == i, term.astype(jnp.float32), terms)
         found = jnp.dot(terms.astype(jnp.bfloat16), chosen, preferred_element_type=jnp.float32)
         ordered = found[0:1] + found[1:2] + found[2:3]
-        out_ref[a] = jnp.where((found[3:4] > 0) & (rank < size), ordered, -1.0)
+        ordered = jnp.where((found[3:4] > 0) & (rank < size), ordered, -1.0)
+        for i in range(splits):
+            out_ref[i * splits + a] = jnp.where(index_ref[1] == i, ordered, -1.0)
 
 
 def local(features, proj_weight, row_cluster, row_rank, owner_slot, tile_size):
     owners, splits = lax.axis_size("dp"), lax.axis_size("split")
+    planes = owners // (2 * splits)
     rows, width = features.shape[0], proj_weight.shape[1]
     block = TILE // splits
     hbm = pl.BlockSpec(memory_space=pltpu.HBM)
@@ -149,6 +153,28 @@
     params = pltpu.CompilerParams(vmem_limit_bytes=32 * 1024 * 1024)
     owner_row = owner_slot.reshape(1, -1)
     member = jnp.where(row_cluster >= 0, row_cluster * TILE + row_rank, -1)
+
+    def device(z, y, core, x):
+        return ((z * splits + y) * 2 + core) * splits + x
+
+    everywhere = [(z, a, b) for z in range(planes) for a in range(splits) for b in range(splits)]
+    diagonals = [
+        [
+            device(z, (g - j) % splits, 1, j) if core else device(z, j, 0, (g - j) % splits)
+            for z in range(planes)
+            for j in range(splits)
+            for core in range(2)
+        ]
+        for g in range(splits)
+    ]
+    sheets = [
+        [device(z, a, core, b) for a in range(splits) for b in range(splits)] for z in range(planes) for core in range(2)
+    ]
+
+    def shift(array, step):
+        pairs = [(device(z, a, 0, b), device(z, a, 0, (b + step) % splits)) for z, a, b in everywhere]
+        pairs += [(device(z, a, 1, b), device(z, (a + step) % splits, 1, b)) for z, a, b in everywhere]
+        return lax.ppermute(array, AXES, pairs)
 
     outgoing = pl.pallas_call(
         lambda *refs: project_kernel(splits, block, *refs),
@@ -164,10 +190,11 @@
         name="project",
     )(features, proj_weight, member.reshape(1, rows), owner_row)
 
-    own = lax.all_to_all(outgoing.reshape(owners, splits // 2, -1), "dp", 0, 0, tiled=True)
+    own = lax.all_to_all(
+        outgoing.reshape(owners, splits // 2, -1), AXES, 0, 0, tiled=True, axis_index_groups=diagonals
+    )
     own = own.transpose(1, 0, 2).reshape(rows // 2, -1)
-    left = lax.ppermute(own, "split", [(i, (i + 1) % splits) for i in range(splits)])
-    right = lax.ppermute(own, "split", [(i, (i - 1) % splits) for i in range(splits)])
+    left, right = shift(own, 1), shift(own, -1)
 
     best = pl.pallas_call(
         lambda *refs: own_kernel(splits, width, owners, *refs),
@@ -178,15 +205,19 @@
         name="own",
         cost_estimate=pl.CostEstimate(flops=2 * rows * rows * width, bytes_accessed=2 << 20, transcendentals=0),
     )(own)
+    owner, x = lax.axis_index("dp"), lax.axis_index("split")
+    z, y, core = owner // (2 * splits), owner // 2 % splits, owner % 2
+    line = jnp.where(core == 0, y, x)
+    index = jnp.stack([(z * splits + line) * 2 + core, line]).astype(jnp.int32)
     best = pl.pallas_call(
         lambda *refs: ring_kernel(splits, width, owners, *refs),
-        out_shape=jax.ShapeDtypeStruct((splits, 1, block), jnp.float32),
+        out_shape=jax.ShapeDtypeStruct((splits * splits, 1, block), jnp.float32),
         in_specs=[smem] + [vmem] * 6,
         out_specs=vmem,
         compiler_params=params,
         name="ring",
-    )(lax.axis_index("dp").reshape(1), owner_row, tile_size.reshape(1, -1), own, left, right, best)
-    return jnp.max(lax.all_to_all(best, "split", 0, 0, tiled=True), axis=0)
+    )(index, owner_row, tile_size.reshape(1, -1), own, left, right, best)
+    return jnp.max(lax.all_to_all(best, AXES, 0, 0, tiled=True, axis_index_groups=sheets), axis=0)
 
 
 def solution(mesh):

time: 110 us -> 109 us (level)
  the two profiles are of different devices: /device:TPU:32 before, /device:TPU:1 now
where the time goes in v4:
time: 109 us; the launch traced here: 108 us
  blocking collectives  82.6 us (76%)
  waiting for transfers between devices  10.6 us (10%)
  Pallas kernels  7.4 us (7%)
  starting transfers between devices  5.28 us (5%)
  other arithmetic  1.39 us (1%)
    all_to_all x1, blocking collectives, local(): lax.all_to_all(outgoing.reshape(owners, splits // 2, -1), AXES, 0, 0, til...  69.2 us
    all_to_all x1, blocking collectives, local(): lax.all_to_all(best, AXES, 0, 0, tiled=True, axis_index_groups=sheets)  13.4 us
    ppermute x2, waiting for transfers between devices, shift(): return lax.ppermute(array, AXES, pairs)  10.6 us
    ppermute x2, starting transfers between devices, shift(): return lax.ppermute(array, AXES, pairs)  5.28 us
    pallas_call x1, Pallas kernels, local(): pl.pallas_call(lambda *refs: project_kernel(splits, block, *refs), out_sh...  3.7 us
    pallas_call x1, Pallas kernels, local(): pl.pallas_call(lambda *refs: ring_kernel(splits, width, owners, *refs), o...  2.83 us
  transfers between devices with their start and end apart: 2, of which 2 were waited for; matrix products, arithmetic and copies ran while one was open for 0% of the time, Pallas kernels for 1%

profile of v4, /device:TPU:1, one launch (start us, length us, event | category | flops | bytes accessed | tf_op | source)
XLA Modules:
  0.0 108.4 jit_solution(8731425933202634886)
XLA Ops:
  0.0 0.7 add_select_fusion
  0.7 0.0 copy-start
  0.7 0.7 copy-done
  1.4 3.7 %project.1 = bf16[256,1664]{1,0:T(8,128)(2,1)S(1)} custom-call(bf16[512,1024]{1,0:T(8,128)(2,1)} %refs_0_.1, bf16[1024,768]{1,0:T(8,128)(2,1)} %refs_1_.1, s32[1,512]{1,0:T(1,128)S(1)} %bitcast.12, s32[1,128]{1,0:T(1,128)S(1)} %bitcast.13), custom_call_target="tpu_custom_call" | custom-call | tf_op jit(solution)/shard_map/project/pallas_call | solution.py:179
  5.1 0.3 reshape.19
  5.4 69.2 %all_to_all.10 = bf16[128,2,1664]{2,1,0:T(2,128)(2,1)S(1)} all-to-all(bf16[128,2,1664]{2,1,0:T(2,128)(2,1)S(1)} %reshape.19), channel_id=1, replica_groups={{0,4,11,29,18,22,25,15,32,36,43,61,50,54,57,47,64,68,75,93,82,86,89,79,..., dimensions={0} | all-to-all | bytes 1703936 | tf_op jit(solution)/shard_map/all_to_all | solution.py:193
  74.6 0.0 copy-start.1
  74.6 0.0 copy-start.2
  74.6 0.1 copy.8
  74.7 1.9 %collective-permute-start.1 = (bf16[256,1664]{1,0:T(8,128)(2,1)S(1)}, bf16[256,1664]{1,0:T(8,128)(2,1)S(1)}, u32[]{:S(2)}, u32[]{:S(2)}) collective-permute-start(bf16[256,1664]{1,0:T(8,128)(2,1)S(1)} %bitcast.8), channel_id=1, source_target_pairs={{0,3},{1,0},{2,1},{3,2},{8,11},{9,8},{10,9},{11,10},{16,19},{17,16... | collective-permute-start | bytes 2555912 | tf_op jit(solution)/shard_map/ppermute | solution.py:177
  76.6 3.4 %collective-permute-start = (bf16[256,1664]{1,0:T(8,128)(2,1)S(1)}, bf16[256,1664]{1,0:T(8,128)(2,1)S(1)}, u32[]{:S(2)}, u32[]{:S(2)}) collective-permute-start(bf16[256,1664]{1,0:T(8,128)(2,1)S(1)} %bitcast.9), channel_id=1, source_target_pairs={{0,1},{1,2},{2,3},{3,0},{8,9},{9,10},{10,11},{11,8},{16,17},{17,18... | collective-permute-start | bytes 2555912 | tf_op jit(solution)/shard_map/ppermute | solution.py:177
  80.0 0.1 pad_add_fusion.refs_0_
  80.1 0.9 own.1.refs_6_
  81.0 7.4 %collective-permute-done.1.refs_5_ = bf16[256,1664]{1,0:T(8,128)(2,1)S(1)} collective-permute-done((bf16[256,1664]{1,0:T(8,128)(2,1)S(1)}, bf16[256,1664]{1,0:T(8,128)(2,1)S(1)}, u32[]{:S(2)}, u32[]{:S(2)}) %collective-permute-start.1) | collective-permute-done | bytes 852000 | tf_op jit(solution)/shard_map/ppermute | solution.py:177
  88.4 3.1 %collective-permute-done.refs_4_ = bf16[256,1664]{1,0:T(8,128)(2,1)S(1)} collective-permute-done((bf16[256,1664]{1,0:T(8,128)(2,1)S(1)}, bf16[256,1664]{1,0:T(8,128)(2,1)S(1)}, u32[]{:S(2)}, u32[]{:S(2)}) %collective-permute-start) | collective-permute-done | bytes 852000 | tf_op jit(solution)/shard_map/ppermute | solution.py:177
  91.6 0.0 copy-done.1
  91.6 0.0 copy-done.2
  91.6 2.8 %ring.1 = f32[16,1,512]{2,1,0:T(1,128)S(1)} custom-call(s32[2]{0:T(128)S(1)} %pad_add_fusion.refs_0_, s32[1,128]{1,0:T(1,128)S(1)} %bitcast.14, s32[1,128]{1,0:T(1,128)S(1)} %bitcast.15, bf16[256,1664]{1,0:T(8,128)(2,1)S(1)} %bitcast.11, bf16[256,1664]{1,0:T(8,128)(2,1)S(1)} %collective-permute-done.refs_4_, ...), custom_call_target="tpu_custom_call" | custom-call | tf_op jit(solution)/shard_map/ring/pallas_call | solution.py:212
  94.4 13.4 %all_to_all.11 = f32[16,1,512]{2,1,0:T(1,128)S(1)} all-to-all(f32[16,1,512]{2,1,0:T(1,128)S(1)} %ring.1), channel_id=1, replica_groups={{0,1,2,3,8,9,10,11,16,17,18,19,24,25,26,27},{4,5,6,7,12,13,14,15,20,21,..., dimensions={0} | all-to-all | bytes 65536 | tf_op jit(solution)/shard_map/all_to_all | solution.py:220
  107.8 0.6 reduce_max.11
Async XLA Ops:
  0.7 0.7 copy-start
  74.6 17.0 %copy-start.1 = (s32[128]{0:T(128)S(1)}, s32[128]{0:T(128)}, u32[]{:S(2)}) copy-start(s32[128]{0:T(128)} %param.10) | copy-start | bytes 1540
  74.6 17.0 %copy-start.2 = (s32[128]{0:T(128)S(1)}, s32[128]{0:T(128)}, u32[]{:S(2)}) copy-start(s32[128]{0:T(128)} %param.11) | copy-start | bytes 1540
  74.7 13.7 %collective-permute-start.1 = (bf16[256,1664]{1,0:T(8,128)(2,1)S(1)}, bf16[256,1664]{1,0:T(8,128)(2,1)S(1)}, u32[]{:S(2)}, u32[]{:S(2)}) collective-permute-start(bf16[256,1664]{1,0:T(8,128)(2,1)S(1)} %bitcast.8), channel_id=1, source_target_pairs={{0,3},{1,0},{2,1},{3,2},{8,11},{9,8},{10,9},{11,10},{16,19},{17,16... | collective-permute-start | bytes 2555912 | tf_op jit(solution)/shard_map/ppermute | solution.py:177
  76.6 14.9 %collective-permute-start = (bf16[256,1664]{1,0:T(8,128)(2,1)S(1)}, bf16[256,1664]{1,0:T(8,128)(2,1)S(1)}, u32[]{:S(2)}, u32[]{:S(2)}) collective-permute-start(bf16[256,1664]{1,0:T(8,128)(2,1)S(1)} %bitcast.9), channel_id=1, source_target_pairs={{0,1},{1,2},{2,3},{3,0},{8,9},{9,10},{10,11},{11,8},{16,17},{17,18... | collective-permute-start | bytes 2555912 | tf_op jit(solution)/shard_map/ppermute | solution.py:177

commit v5 on v4

v5 whole, which is shorter than its diff:
```python
import jax
import jax.numpy as jnp
from jax import lax
from jax.experimental import pallas as pl
from jax.experimental.pallas import tpu as pltpu
from jax.sharding import PartitionSpec as P

TILE = 2048
EPS = 1e-06
AXES = ("dp", "split")
NT = (((1,), (1,)), ((), ()))
FAR = 1e9


def iota(shape, dim):
    return lax.broadcasted_iota(jnp.int32, shape, dim)


def bf16(mask_or_int):
    return mask_or_int.astype(jnp.float32).astype(jnp.bfloat16)


def project_kernel(
    splits, block, features_hbm, weight_hbm, member_ref, owner_ref, other_ref, mine_ref, features, weight, semaphores
):
    steps = 4
    part = features.shape[1] // steps
    spans = [slice(i * part, (i + 1) * part) for i in range(steps)]
    pairs = []
    for span in spans:
        pairs.append((weight_hbm.at[span, :], weight.at[span, :]))
        pairs.append((features_hbm.at[:, span], features.at[:, span]))
    copies = [pltpu.make_async_copy(*pair, semaphores.at[i]) for i, pair in enumerate(pairs)]
    for copy in copies:
        copy.start()
    member = member_ref[...]
    clusters, rows, width = owner_ref.shape[1], member.shape[1], weight.shape[1]
    chips = mine_ref.shape[0]
    cluster, rank = member // TILE, member % TILE
    owner = bf16(jnp.broadcast_to(owner_ref[...], (8, clusters)))
    named = bf16(iota((clusters, rows), 0) == cluster)
    slot = jnp.dot(owner, named, preferred_element_type=jnp.float32)[0:1].astype(jnp.int32)
    core = lax.axis_index("dp") % 2
    place = rank // block * chips + slot // 2
    high, low = (rank + 1) // 16, (rank + 1) % 16
    lane = iota((128, rows), 0)
    digits = bf16(jnp.where(lane // 2 == rank // block, jnp.where(lane % 2 == 0, high, low), 0))
    outs = []
    for out_ref, to in ((other_ref, 1 - core), (mine_ref, core)):
        target = jnp.where((member >= 0) & (slot % 2 == to), place, -1)
        chosen = bf16(iota((splits * chips, rows), 0) == target)
        outs.append((out_ref, chosen))
        anywhere = chosen[:chips]
        for a in range(1, splits):
            anywhere = anywhere + chosen[a * chips : (a + 1) * chips]
        numbers = lax.dot_general(anywhere, digits, NT, preferred_element_type=jnp.float32)
        out_ref[:, splits * width :] = numbers.astype(jnp.bfloat16)

    projected = jnp.zeros((rows, width), jnp.float32)
    for i, span in enumerate(spans):
        copies[2 * i].wait()
        copies[2 * i + 1].wait()
        projected += jnp.dot(features[:, span], weight[span, :], preferred_element_type=jnp.float32)
    normed = projected * lax.rsqrt(jnp.sum(projected * projected, axis=1, keepdims=True) + EPS)
    normed = normed.astype(jnp.bfloat16)
    for out_ref, chosen in outs:
        sent = jnp.dot(chosen, normed, preferred_element_type=jnp.float32).astype(jnp.bfloat16)
        for a in range(splits):
            out_ref[:, a * width : (a + 1) * width] = sent[a * chips : (a + 1) * chips]


def merge_kernel(first_ref, second_ref, out_ref):
    out_ref[:, 0, :] = first_ref[...]
    out_ref[:, 1, :] = second_ref[...]


class Members:
    def __init__(self, ref, width, splits):
        self.ref, self.width, self.splits, self.digits = ref, width, splits, ref[:, splits * width :]

    def rows(self, index):
        return self.ref[:, index * self.width : (index + 1) * self.width]

    def down(self):
        step = self.ref.shape[0]
        lane, digit = iota((128, self.splits * step), 1) // step, iota((128, self.splits * step), 0)
        weights = bf16(jnp.where(digit == 2 * lane, 16, jnp.where(digit == 2 * lane + 1, 1, 0)))
        return jnp.dot(self.digits, weights, preferred_element_type=jnp.float32)

    def along(self):
        line, digit = iota((8, 128), 0), iota((8, 128), 1)
        weights = bf16(jnp.where(digit == 2 * line, 16, jnp.where(digit == 2 * line + 1, 1, 0)))
        return lax.dot_general(weights, self.digits, NT, preferred_element_type=jnp.float32)

    def stacked(self):
        return jnp.concatenate([self.rows(a) for a in range(self.splits)], axis=0)


def earlier_max(best, members, queries):
    splits, step = len(best), queries.ref.shape[0]
    later, numbers = queries.stacked(), queries.along()
    for part in members:
        scores = lax.dot_general(part.stacked(), later, NT, preferred_element_type=jnp.float32)
        down = part.down()
        down = jnp.where(down > 0, down, FAR)
        for b in range(splits):
            number = down[:, b * step : (b + 1) * step]
            for a in range(b, splits):
                tile = scores[b * step : (b + 1) * step, a * step : (a + 1) * step]
                found = jnp.where(number < numbers[a : a + 1], tile, -1.0)
                best[a] = jnp.maximum(best[a], jnp.max(found.reshape(-1, 8, step), axis=0))
    return best


def own_kernel(splits, width, step, own_ref, out_ref):
    own = Members(own_ref, width, splits)
    best = [jnp.full((8, step), -1.0, jnp.float32) for _ in range(splits)]
    best = earlier_max(best, [own], own)
    for a in range(splits):
        out_ref[:, a * step : (a + 1) * step] = best[a]


def ring_kernel(splits, width, step, index_ref, owner_ref, size_ref, own_ref, left_ref, right_ref, best_ref, out_ref):
    block = out_ref.shape[2]
    own, left, right = [Members(ref, width, splits) for ref in (own_ref, left_ref, right_ref)]
    own_best = [best_ref[:, a * step : (a + 1) * step] for a in range(splits)]
    own_best = earlier_max(own_best, [left, right], own)
    left_best = [jnp.full((8, step), -1.0, jnp.float32) for _ in range(splits)]
    left_best = earlier_max(left_best, [right], left)
    own_down, left_down = own.down(), left.down()

    size = jnp.sum(jnp.where(owner_ref[...] == index_ref[0], size_ref[...], 0), axis=1, keepdims=True)
    for a in range(splits):
        rank = a * block + iota((1, block), 1)
        target = (rank + 1).astype(jnp.float32)
        span = slice(a * step, (a + 1) * step)
        column = jnp.concatenate([own_down[:, span], left_down[:, span]], axis=0)
        chosen = jnp.concatenate(
            [bf16(column == target[:, i * step : (i + 1) * step]) for i in range(block // step)], axis=1
        )
        best = jnp.concatenate(
            [jnp.max(own_best[a], axis=0, keepdims=True), jnp.max(left_best[a], axis=0, keepdims=True)], axis=1
        )
        first = best.astype(jnp.bfloat16)
        rest = best - first.astype(jnp.float32)
        second = rest.astype(jnp.bfloat16)
        third = (rest - second.astype(jnp.float32)).astype(jnp.bfloat16)
        line = iota((8, best.shape[1]), 0)
        terms = jnp.ones(line.shape, jnp.float32)
        for i, term in enumerate((first, second, third)):
            terms = jnp.where(line == i, term.astype(jnp.float32), terms)
        found = jnp.dot(terms.astype(jnp.bfloat16), chosen, preferred_element_type=jnp.float32)
        ordered = found[0:1] + found[1:2] + found[2:3]
        ordered = jnp.where((found[3:4] > 0) & (rank < size), ordered, -1.0)
        for i in range(splits):
            out_ref[i * splits + a] = jnp.where(index_ref[1] == i, ordered, -1.0)


def local(features, proj_weight, row_cluster, row_rank, owner_slot, tile_size):
    owners, splits = lax.axis_size("dp"), lax.axis_size("split")
    planes = owners // (2 * splits)
    rows, width = features.shape[0], proj_weight.shape[1]
    block = TILE // splits
    hbm = pl.BlockSpec(memory_space=pltpu.HBM)
    vmem = pl.BlockSpec(memory_space=pltpu.VMEM)
    smem = pl.BlockSpec(memory_space=pltpu.SMEM)
    params = pltpu.CompilerParams(vmem_limit_bytes=32 * 1024 * 1024)
    owner_row = owner_slot.reshape(1, -1)
    member = jnp.where(row_cluster >= 0, row_cluster * TILE + row_rank, -1)

    def device(z, y, core, x):
        return ((z * splits + y) * 2 + core) * splits + x

    everywhere = [(z, a, b) for z in range(planes) for a in range(splits) for b in range(splits)]
    columns = [[device(z, j, 0, g) for z in range(planes) for j in range(splits)] for g in range(splits)]
    columns += [[device(z, g, 1, j) for z in range(planes) for j in range(splits)] for g in range(splits)]
    sheets = [
        [device(z, a, core, b) for a in range(splits) for b in range(splits)] for z in range(planes) for core in range(2)
    ]

    def shift(array, step):
        pairs = [(device(z, a, 0, b), device(z, a, 0, (b + step) % splits)) for z, a, b in everywhere]
        pairs += [(device(z, a, 1, b), device(z, (a + step) % splits, 1, b)) for z, a, b in everywhere]
        return lax.ppermute(array, AXES, pairs)

    chips = owners // 2
    other, mine = pl.pallas_call(
        lambda *refs: project_kernel(splits, block, *refs),
        out_shape=[jax.ShapeDtypeStruct((chips, splits * width + 128), jnp.bfloat16)] * 2,
        in_specs=[hbm] * 2 + [vmem] * 2,
        out_specs=[vmem] * 2,
        scratch_shapes=[
            pltpu.VMEM(features.shape, jnp.bfloat16),
            pltpu.VMEM(proj_weight.shape, jnp.bfloat16),
            pltpu.SemaphoreType.DMA((8,)),
        ],
        compiler_params=pltpu.CompilerParams(vmem_limit_bytes=55200000),
        name="project",
    )(features, proj_weight, member.reshape(1, rows), owner_row)

    swap = [(device(z, a, core, b), device(z, a, 1 - core, b)) for z, a, b in everywhere for core in range(2)]
    outgoing = pl.pallas_call(
        merge_kernel,
        out_shape=jax.ShapeDtypeStruct((chips, 2, splits * width + 128), jnp.bfloat16),
        in_specs=[vmem] * 2,
        out_specs=vmem,
        compiler_params=params,
        name="merge",
    )(mine, lax.ppermute(other, AXES, swap))
    own = lax.all_to_all(outgoing, AXES, 0, 0, tiled=True, axis_index_groups=columns).reshape(owners, -1)
    left, right = shift(own, 1), shift(own, -1)

    best = pl.pallas_call(
        lambda *refs: own_kernel(splits, width, owners, *refs),
        out_shape=jax.ShapeDtypeStruct((8, splits * owners), jnp.float32),
        in_specs=[vmem],
        out_specs=vmem,
        compiler_params=params,
        name="own",
        cost_estimate=pl.CostEstimate(flops=2 * rows * rows * width, bytes_accessed=2 << 20, transcendentals=0),
    )(own)
    owner, x = lax.axis_index("dp"), lax.axis_index("split")
    z, y, core = owner // (2 * splits), owner // 2 % splits, owner % 2
    line = jnp.where(core == 0, y, x)
    index = jnp.stack([(z * splits + line) * 2 + core, line]).astype(jnp.int32)
    best = pl.pallas_call(
        lambda *refs: ring_kernel(splits, width, owners, *refs),
        out_shape=jax.ShapeDtypeStruct((splits * splits, 1, block), jnp.float32),
        in_specs=[smem] + [vmem] * 6,
        out_specs=vmem,
        compiler_params=params,
        name="ring",
    )(index, owner_row, tile_size.reshape(1, -1), own, left, right, best)
    return jnp.max(lax.all_to_all(best, AXES, 0, 0, tiled=True, axis_index_groups=sheets), axis=0)


def solution(mesh):
    return jax.shard_map(
        local,
        mesh=mesh,
        in_specs=(P(("dp", "split"), None), P(), P(("dp", "split")), P(("dp", "split")), P(), P()),
        out_specs=P("dp", "split"),
        check_vma=False,
    )
```

time: 109 us -> 108 us (level)
  the two profiles are of different devices: /device:TPU:1 before, /device:TPU:2 now
where the time goes in v5:
time: 108 us
  blocking collectives  77.8 us (72%)
  waiting for transfers between devices  12.4 us (11%)
  starting transfers between devices  7.76 us (7%)
  Pallas kernels  7.23 us (7%)
  other arithmetic  1.39 us (1%)
    all_to_all x1, blocking collectives, local(): lax.all_to_all(outgoing, AXES, 0, 0, tiled=True, axis_index_groups=columns)  64.1 us
    all_to_all x1, blocking collectives, local(): lax.all_to_all(best, AXES, 0, 0, tiled=True, axis_index_groups=sheets)  13.7 us
    ppermute x2, waiting for transfers between devices, shift(): return lax.ppermute(array, AXES, pairs)  10.7 us
    ppermute x2, starting transfers between devices, shift(): return lax.ppermute(array, AXES, pairs)  5.84 us
    pallas_call x1, Pallas kernels, local(): pl.pallas_call(lambda *refs: project_kernel(splits, block, *refs), out_sh...  3.65 us
    pallas_call x1, Pallas kernels, local(): pl.pallas_call(lambda *refs: ring_kernel(splits, width, owners, *refs), o...  2.47 us
  transfers between devices with their start and end apart: 3, of which 3 were waited for; matrix products, arithmetic and copies ran while one was open for 0% of the time, Pallas kernels for 1%

profile of v5, /device:TPU:2, one launch (start us, length us, event | category | flops | bytes accessed | tf_op | source)
XLA Modules:
  0.0 107.7 jit_solution(10589351282696480257)
XLA Ops:
  0.0 0.7 add_select_fusion
  0.7 0.0 copy-start
  0.7 0.7 copy-done
  1.4 3.7 %project.1 = (bf16[64,3200]{1,0:T(8,128)(2,1)S(1)}, bf16[64,3200]{1,0:T(8,128)(2,1)S(1)}) custom-call(bf16[512,1024]{1,0:T(8,128)(2,1)} %refs_0_.1, bf16[1024,768]{1,0:T(8,128)(2,1)} %refs_1_.1, s32[1,512]{1,0:T(1,128)S(1)} %bitcast.6, s32[1,128]{1,0:T(1,128)S(1)} %bitcast.7), custom_call_target="tpu_custom_call" | custom-call | tf_op jit(solution)/shard_map/project/pallas_call | solution.py:187
  5.0 1.9 %collective-permute-start = (bf16[64,3200]{1,0:T(8,128)(2,1)S(1)}, bf16[64,3200]{1,0:T(8,128)(2,1)S(1)}, u32[]{:S(2)}, u32[]{:S(2)}) collective-permute-start(bf16[64,3200]{1,0:T(8,128)(2,1)S(1)} %get-tuple-element.8), channel_id=1, source_target_pairs={{0,4},{4,0},{1,5},{5,1},{2,6},{6,2},{3,7},{7,3},{8,12},{12,8},{9,1... | collective-permute-start | bytes 1228808 | tf_op jit(solution)/shard_map/ppermute | solution.py:209
  6.9 1.7 %collective-permute-done.second_ref = bf16[64,3200]{1,0:T(8,128)(2,1)S(1)} collective-permute-done((bf16[64,3200]{1,0:T(8,128)(2,1)S(1)}, bf16[64,3200]{1,0:T(8,128)(2,1)S(1)}, u32[]{:S(2)}, u32[]{:S(2)}) %collective-permute-start) | collective-permute-done | bytes 409632 | tf_op jit(solution)/shard_map/ppermute | solution.py:209
  8.7 0.4 merge.1
  9.1 64.1 %all_to_all.10 = bf16[64,2,3200]{2,1,0:T(2,128)(2,1)S(1)} all-to-all(bf16[64,2,3200]{2,1,0:T(2,128)(2,1)S(1)} %merge.1), channel_id=1, replica_groups={{0,8,16,24,32,40,48,56,64,72,80,88,96,104,112,120,128,136,144,152,160,1..., dimensions={0} | all-to-all | bytes 1638400 | tf_op jit(solution)/shard_map/all_to_all | solution.py:210
  73.2 0.0 copy-start.1
  73.2 0.0 copy-start.2
  73.2 0.3 reshape.16.refs_0_.refs_3_
  73.5 2.5 %collective-permute-start.2 = (bf16[128,3200]{1,0:T(8,128)(2,1)S(1)}, bf16[128,3200]{1,0:T(8,128)(2,1)S(1)}, u32[]{:S(2)}, u32[]{:S(2)}) collective-permute-start(bf16[128,3200]{1,0:T(8,128)(2,1)S(1)} %reshape.16.refs_0_.refs_3_), channel_id=1, source_target_pairs={{0,3},{1,0},{2,1},{3,2},{8,11},{9,8},{10,9},{11,10},{16,19},{17,16... | collective-permute-start | bytes 2457608 | tf_op jit(solution)/shard_map/ppermute | solution.py:184
  76.0 3.4 %collective-permute-start.1 = (bf16[128,3200]{1,0:T(8,128)(2,1)S(1)}, bf16[128,3200]{1,0:T(8,128)(2,1)S(1)}, u32[]{:S(2)}, u32[]{:S(2)}) collective-permute-start(bf16[128,3200]{1,0:T(8,128)(2,1)S(1)} %reshape.16.refs_0_.refs_3_), channel_id=1, source_target_pairs={{0,1},{1,2},{2,3},{3,0},{8,9},{9,10},{10,11},{11,8},{16,17},{17,18... | collective-permute-start | bytes 2457608 | tf_op jit(solution)/shard_map/ppermute | solution.py:184
  79.4 0.1 pad_add_fusion.refs_0_
  79.5 0.7 own.1.refs_6_
  80.2 7.5 %collective-permute-done.2.refs_5_ = bf16[128,3200]{1,0:T(8,128)(2,1)S(1)} collective-permute-done((bf16[128,3200]{1,0:T(8,128)(2,1)S(1)}, bf16[128,3200]{1,0:T(8,128)(2,1)S(1)}, u32[]{:S(2)}, u32[]{:S(2)}) %collective-permute-start.2) | collective-permute-done | bytes 819232 | tf_op jit(solution)/shard_map/ppermute | solution.py:184
  87.7 3.2 %collective-permute-done.1.refs_4_ = bf16[128,3200]{1,0:T(8,128)(2,1)S(1)} collective-permute-done((bf16[128,3200]{1,0:T(8,128)(2,1)S(1)}, bf16[128,3200]{1,0:T(8,128)(2,1)S(1)}, u32[]{:S(2)}, u32[]{:S(2)}) %collective-permute-start.1) | collective-permute-done | bytes 819232 | tf_op jit(solution)/shard_map/ppermute | solution.py:184
  90.9 0.0 copy-done.1
  90.9 0.0 copy-done.2
  90.9 2.5 %ring.1 = f32[16,1,512]{2,1,0:T(1,128)S(1)} custom-call(s32[2]{0:T(128)S(1)} %pad_add_fusion.refs_0_, s32[1,128]{1,0:T(1,128)S(1)} %bitcast.8, s32[1,128]{1,0:T(1,128)S(1)} %bitcast.9, bf16[128,3200]{1,0:T(8,128)(2,1)S(1)} %reshape.16.refs_0_.refs_3_, bf16[128,3200]{1,0:T(8,128)(2,1)S(1)} %collective-permute-done.1.refs_4_, ...), custom_call_target="tpu_custom_call" | custom-call | tf_op jit(solution)/shard_map/ring/pallas_call | solution.py:226
  93.4 13.7 %all_to_all.11 = f32[16,1,512]{2,1,0:T(1,128)S(1)} all-to-all(f32[16,1,512]{2,1,0:T(1,128)S(1)} %ring.1), channel_id=1, replica_groups={{0,1,2,3,8,9,10,11,16,17,18,19,24,25,26,27},{4,5,6,7,12,13,14,15,20,21,..., dimensions={0} | all-to-all | bytes 65536 | tf_op jit(solution)/shard_map/all_to_all | solution.py:234
  107.1 0.6 reduce_max.11
Async XLA Ops:
  0.7 0.7 copy-start
  5.0 3.6 %collective-permute-start = (bf16[64,3200]{1,0:T(8,128)(2,1)S(1)}, bf16[64,3200]{1,0:T(8,128)(2,1)S(1)}, u32[]{:S(2)}, u32[]{:S(2)}) collective-permute-start(bf16[64,3200]{1,0:T(8,128)(2,1)S(1)} %get-tuple-element.8), channel_id=1, source_target_pairs={{0,4},{4,0},{1,5},{5,1},{2,6},{6,2},{3,7},{7,3},{8,12},{12,8},{9,1... | collective-permute-start | bytes 1228808 | tf_op jit(solution)/shard_map/ppermute | solution.py:209
  73.2 17.7 %copy-start.1 = (s32[128]{0:T(128)S(1)}, s32[128]{0:T(128)}, u32[]{:S(2)}) copy-start(s32[128]{0:T(128)} %param.10) | copy-start | bytes 1540
  73.2 17.7 %copy-start.2 = (s32[128]{0:T(128)S(1)}, s32[128]{0:T(128)}, u32[]{:S(2)}) copy-start(s32[128]{0:T(128)} %param.11) | copy-start | bytes 1540
  73.5 14.2 %collective-permute-start.2 = (bf16[128,3200]{1,0:T(8,128)(2,1)S(1)}, bf16[128,3200]{1,0:T(8,128)(2,1)S(1)}, u32[]{:S(2)}, u32[]{:S(2)}) collective-permute-start(bf16[128,3200]{1,0:T(8,128)(2,1)S(1)} %reshape.16.refs_0_.refs_3_), channel_id=1, source_target_pairs={{0,3},{1,0},{2,1},{3,2},{8,11},{9,8},{10,9},{11,10},{16,19},{17,16... | collective-permute-start | bytes 2457608 | tf_op jit(solution)/shard_map/ppermute | solution.py:184
  76.0 14.9 %collective-permute-start.1 = (bf16[128,3200]{1,0:T(8,128)(2,1)S(1)}, bf16[128,3200]{1,0:T(8,128)(2,1)S(1)}, u32[]{:S(2)}, u32[]{:S(2)}) collective-permute-start(bf16[128,3200]{1,0:T(8,128)(2,1)S(1)} %reshape.16.refs_0_.refs_3_), channel_id=1, source_target_pairs={{0,1},{1,2},{2,3},{3,0},{8,9},{9,10},{10,11},{11,8},{16,17},{17,18... | collective-permute-start | bytes 2457608 | tf_op jit(solution)/shard_map/ppermute | solution.py:184

commit v6 on v5

--- a/solution.py
+++ b/solution.py
@@ -41,18 +41,15 @@
     named = bf16(iota((clusters, rows), 0) == cluster)
     slot = jnp.dot(owner, named, preferred_element_type=jnp.float32)[0:1].astype(jnp.int32)
     core = lax.axis_index("dp") % 2
-    place = rank // block * chips + slot // 2
+    here = jnp.where(slot % 2 == core, 1, 0)
+    target = jnp.where(member >= 0, (here * splits + rank // block) * chips + slot // 2, -1)
+    chosen = bf16(iota((2 * splits * chips, rows), 0) == target)
     high, low = (rank + 1) // 16, (rank + 1) % 16
     lane = iota((128, rows), 0)
     digits = bf16(jnp.where(lane // 2 == rank // block, jnp.where(lane % 2 == 0, high, low), 0))
-    outs = []
-    for out_ref, to in ((other_ref, 1 - core), (mine_ref, core)):
-        target = jnp.where((member >= 0) & (slot % 2 == to), place, -1)
-        chosen = bf16(iota((splits * chips, rows), 0) == target)
-        outs.append((out_ref, chosen))
-        anywhere = chosen[:chips]
-        for a in range(1, splits):
-            anywhere = anywhere + chosen[a * chips : (a + 1) * chips]
+    for i, out_ref in enumerate((other_ref, mine_ref)):
+        parts = [chosen[(i * splits + a) * chips : (i * splits + a + 1) * chips] for a in range(splits)]
+        anywhere = (parts[0] + parts[1]) + (parts[2] + parts[3])
         numbers = lax.dot_general(anywhere, digits, NT, preferred_element_type=jnp.float32)
         out_ref[:, splits * width :] = numbers.astype(jnp.bfloat16)
 
@@ -63,10 +60,11 @@
         projected += jnp.dot(features[:, span], weight[span, :], preferred_element_type=jnp.float32)
     normed = projected * lax.rsqrt(jnp.sum(projected * projected, axis=1, keepdims=True) + EPS)
     normed = normed.astype(jnp.bfloat16)
-    for out_ref, chosen in outs:
-        sent = jnp.dot(chosen, normed, preferred_element_type=jnp.float32).astype(jnp.bfloat16)
+    sent = jnp.dot(chosen, normed, preferred_element_type=jnp.float32).astype(jnp.bfloat16)
+    for i, out_ref in enumerate((other_ref, mine_ref)):
         for a in range(splits):
-            out_ref[:, a * width : (a + 1) * width] = sent[a * chips : (a + 1) * chips]
+            start = (i * splits + a) * chips
+            out_ref[:, a * width : (a + 1) * width] = sent[start : start + chips]
 
 
 def merge_kernel(first_ref, second_ref, out_ref):
@@ -120,11 +118,18 @@
         out_ref[:, a * step : (a + 1) * step] = best[a]
 
 
+def side_kernel(splits, width, step, own_ref, side_ref, best_ref, out_ref):
+    own, side = [Members(ref, width, splits) for ref in (own_ref, side_ref)]
+    best = earlier_max([best_ref[:, a * step : (a + 1) * step] for a in range(splits)], [side], own)
+    for a in range(splits):
+        out_ref[:, a * step : (a + 1) * step] = best[a]
+
+
 def ring_kernel(splits, width, step, index_ref, owner_ref, size_ref, own_ref, left_ref, right_ref, best_ref, out_ref):
     block = out_ref.shape[2]
     own, left, right = [Members(ref, width, splits) for ref in (own_ref, left_ref, right_ref)]
     own_best = [best_ref[:, a * step : (a + 1) * step] for a in range(splits)]
-    own_best = earlier_max(own_best, [left, right], own)
+    own_best = earlier_max(own_best, [left], own)
     left_best = [jnp.full((8, step), -1.0, jnp.float32) for _ in range(splits)]
     left_best = earlier_max(left_best, [right], left)
     own_down, left_down = own.down(), left.down()
@@ -219,6 +224,15 @@
         name="own",
         cost_estimate=pl.CostEstimate(flops=2 * rows * rows * width, bytes_accessed=2 << 20, transcendentals=0),
     )(own)
+    best = pl.pallas_call(
+        lambda *refs: side_kernel(splits, width, owners, *refs),
+        out_shape=jax.ShapeDtypeStruct((8, splits * owners), jnp.float32),
+        in_specs=[vmem] * 3,
+        out_specs=vmem,
+        compiler_params=params,
+        name="side",
+        cost_estimate=pl.CostEstimate(flops=2 * rows * rows * width, bytes_accessed=2 << 20, transcendentals=0),
+    )(own, right, best)
     owner, x = lax.axis_index("dp"), lax.axis_index("split")
     z, y, core = owner // (2 * splits), owner // 2 % splits, owner % 2
     line = jnp.where(core == 0, y, x)

time: 108 us -> 107 us (level)
  no operation moved by 1% of the time
where the time goes in v6:
time: 107 us
  blocking collectives  77.8 us (73%)
  waiting for transfers between devices  11.7 us (11%)
  starting transfers between devices  7.76 us (7%)
  Pallas kernels  7.26 us (7%)
  other arithmetic  1.39 us (1%)
    all_to_all x1, blocking collectives, local(): lax.all_to_all(outgoing, AXES, 0, 0, tiled=True, axis_index_groups=columns)  64.1 us
    all_to_all x1, blocking collectives, local(): lax.all_to_all(best, AXES, 0, 0, tiled=True, axis_index_groups=sheets)  13.8 us
    ppermute x2, waiting for transfers between devices, shift(): return lax.ppermute(array, AXES, pairs)  10 us
    ppermute x2, starting transfers between devices, shift(): return lax.ppermute(array, AXES, pairs)  5.84 us
    pallas_call x1, Pallas kernels, local(): pl.pallas_call(lambda *refs: project_kernel(splits, block, *refs), out_sh...  3.41 us
  transfers between devices with their start and end apart: 3, of which 3 were waited for; matrix products, arithmetic and copies ran while one was open for 0% of the time, Pallas kernels for 1%

profile of v6, /device:TPU:2, one launch (start us, length us, event | category | flops | bytes accessed | tf_op | source)
XLA Modules:
  0.0 107.1 jit_solution(9280468447749394215)
XLA Ops:
  0.0 0.7 add_select_fusion
  0.7 0.0 copy-start
  0.7 0.7 copy-done
  1.4 3.4 %project.1 = (bf16[64,3200]{1,0:T(8,128)(2,1)S(1)}, bf16[64,3200]{1,0:T(8,128)(2,1)S(1)}) custom-call(bf16[512,1024]{1,0:T(8,128)(2,1)} %refs_0_.1, bf16[1024,768]{1,0:T(8,128)(2,1)} %refs_1_.1, s32[1,512]{1,0:T(1,128)S(1)} %bitcast.6, s32[1,128]{1,0:T(1,128)S(1)} %bitcast.7), custom_call_target="tpu_custom_call" | custom-call | tf_op jit(solution)/shard_map/project/pallas_call | solution.py:192
  4.8 1.9 %collective-permute-start = (bf16[64,3200]{1,0:T(8,128)(2,1)S(1)}, bf16[64,3200]{1,0:T(8,128)(2,1)S(1)}, u32[]{:S(2)}, u32[]{:S(2)}) collective-permute-start(bf16[64,3200]{1,0:T(8,128)(2,1)S(1)} %get-tuple-element.8), channel_id=1, source_target_pairs={{0,4},{4,0},{1,5},{5,1},{2,6},{6,2},{3,7},{7,3},{8,12},{12,8},{9,1... | collective-permute-start | bytes 1228808 | tf_op jit(solution)/shard_map/ppermute | solution.py:214
  6.7 1.7 %collective-permute-done.second_ref = bf16[64,3200]{1,0:T(8,128)(2,1)S(1)} collective-permute-done((bf16[64,3200]{1,0:T(8,128)(2,1)S(1)}, bf16[64,3200]{1,0:T(8,128)(2,1)S(1)}, u32[]{:S(2)}, u32[]{:S(2)}) %collective-permute-start) | collective-permute-done | bytes 409632 | tf_op jit(solution)/shard_map/ppermute | solution.py:214
  8.4 0.4 merge.1
  8.8 64.1 %all_to_all.10 = bf16[64,2,3200]{2,1,0:T(2,128)(2,1)S(1)} all-to-all(bf16[64,2,3200]{2,1,0:T(2,128)(2,1)S(1)} %merge.1), channel_id=1, replica_groups={{0,8,16,24,32,40,48,56,64,72,80,88,96,104,112,120,128,136,144,152,160,1..., dimensions={0} | all-to-all | bytes 1638400 | tf_op jit(solution)/shard_map/all_to_all | solution.py:215
  72.9 0.3 reshape.16.refs_0_.refs_3_
  73.2 2.5 %collective-permute-start.2 = (bf16[128,3200]{1,0:T(8,128)(2,1)S(1)}, bf16[128,3200]{1,0:T(8,128)(2,1)S(1)}, u32[]{:S(2)}, u32[]{:S(2)}) collective-permute-start(bf16[128,3200]{1,0:T(8,128)(2,1)S(1)} %reshape.16.refs_0_.refs_3_), channel_id=1, source_target_pairs={{0,3},{1,0},{2,1},{3,2},{8,11},{9,8},{10,9},{11,10},{16,19},{17,16... | collective-permute-start | bytes 2457608 | tf_op jit(solution)/shard_map/ppermute | solution.py:189
  75.7 3.4 %collective-permute-start.1 = (bf16[128,3200]{1,0:T(8,128)(2,1)S(1)}, bf16[128,3200]{1,0:T(8,128)(2,1)S(1)}, u32[]{:S(2)}, u32[]{:S(2)}) collective-permute-start(bf16[128,3200]{1,0:T(8,128)(2,1)S(1)} %reshape.16.refs_0_.refs_3_), channel_id=1, source_target_pairs={{0,1},{1,2},{2,3},{3,0},{8,9},{9,10},{10,11},{11,8},{16,17},{17,18... | collective-permute-start | bytes 2457608 | tf_op jit(solution)/shard_map/ppermute | solution.py:189
  79.1 0.1 pad_add_fusion.refs_0_
  79.2 0.0 copy-start.1
  79.2 0.0 copy-start.2
  79.2 0.7 own.1.refs_2_
  79.9 7.5 %collective-permute-done.2.refs_1_.refs_5_ = bf16[128,3200]{1,0:T(8,128)(2,1)S(1)} collective-permute-done((bf16[128,3200]{1,0:T(8,128)(2,1)S(1)}, bf16[128,3200]{1,0:T(8,128)(2,1)S(1)}, u32[]{:S(2)}, u32[]{:S(2)}) %collective-permute-start.2) | collective-permute-done | bytes 819232 | tf_op jit(solution)/shard_map/ppermute | solution.py:189
  87.5 0.7 side.1.refs_6_
  88.2 2.5 %collective-permute-done.1.refs_4_ = bf16[128,3200]{1,0:T(8,128)(2,1)S(1)} collective-permute-done((bf16[128,3200]{1,0:T(8,128)(2,1)S(1)}, bf16[128,3200]{1,0:T(8,128)(2,1)S(1)}, u32[]{:S(2)}, u32[]{:S(2)}) %collective-permute-start.1) | collective-permute-done | bytes 819232 | tf_op jit(solution)/shard_map/ppermute | solution.py:189
  90.6 0.0 copy-done.1
  90.6 0.0 copy-done.2
  90.6 2.0 %ring.1 = f32[16,1,512]{2,1,0:T(1,128)S(1)} custom-call(s32[2]{0:T(128)S(1)} %pad_add_fusion.refs_0_, s32[1,128]{1,0:T(1,128)S(1)} %bitcast.8, s32[1,128]{1,0:T(1,128)S(1)} %bitcast.9, bf16[128,3200]{1,0:T(8,128)(2,1)S(1)} %reshape.16.refs_0_.refs_3_, bf16[128,3200]{1,0:T(8,128)(2,1)S(1)} %collective-permute-done.1.refs_4_, ...), custom_call_target="tpu_custom_call" | custom-call | tf_op jit(solution)/shard_map/ring/pallas_call | solution.py:240
  92.7 13.8 %all_to_all.11 = f32[16,1,512]{2,1,0:T(1,128)S(1)} all-to-all(f32[16,1,512]{2,1,0:T(1,128)S(1)} %ring.1), channel_id=1, replica_groups={{0,1,2,3,8,9,10,11,16,17,18,19,24,25,26,27},{4,5,6,7,12,13,14,15,20,21,..., dimensions={0} | all-to-all | bytes 65536 | tf_op jit(solution)/shard_map/all_to_all | solution.py:248
  106.4 0.6 reduce_max.11
Async XLA Ops:
  0.7 0.7 copy-start
  4.8 3.6 %collective-permute-start = (bf16[64,3200]{1,0:T(8,128)(2,1)S(1)}, bf16[64,3200]{1,0:T(8,128)(2,1)S(1)}, u32[]{:S(2)}, u32[]{:S(2)}) collective-permute-start(bf16[64,3200]{1,0:T(8,128)(2,1)S(1)} %get-tuple-element.8), channel_id=1, source_target_pairs={{0,4},{4,0},{1,5},{5,1},{2,6},{6,2},{3,7},{7,3},{8,12},{12,8},{9,1... | collective-permute-start | bytes 1228808 | tf_op jit(solution)/shard_map/ppermute | solution.py:214
  73.2 14.2 %collective-permute-start.2 = (bf16[128,3200]{1,0:T(8,128)(2,1)S(1)}, bf16[128,3200]{1,0:T(8,128)(2,1)S(1)}, u32[]{:S(2)}, u32[]{:S(2)}) collective-permute-start(bf16[128,3200]{1,0:T(8,128)(2,1)S(1)} %reshape.16.refs_0_.refs_3_), channel_id=1, source_target_pairs={{0,3},{1,0},{2,1},{3,2},{8,11},{9,8},{10,9},{11,10},{16,19},{17,16... | collective-permute-start | bytes 2457608 | tf_op jit(solution)/shard_map/ppermute | solution.py:189
  75.7 14.9 %collective-permute-start.1 = (bf16[128,3200]{1,0:T(8,128)(2,1)S(1)}, bf16[128,3200]{1,0:T(8,128)(2,1)S(1)}, u32[]{:S(2)}, u32[]{:S(2)}) collective-permute-start(bf16[128,3200]{1,0:T(8,128)(2,1)S(1)} %reshape.16.refs_0_.refs_3_), channel_id=1, source_target_pairs={{0,1},{1,2},{2,3},{3,0},{8,9},{9,10},{10,11},{11,8},{16,17},{17,18... | collective-permute-start | bytes 2457608 | tf_op jit(solution)/shard_map/ppermute | solution.py:189
  79.2 11.4 %copy-start.1 = (s32[128]{0:T(128)S(1)}, s32[128]{0:T(128)}, u32[]{:S(2)}) copy-start(s32[128]{0:T(128)} %param.10) | copy-start | bytes 1540
  79.2 11.4 %copy-start.2 = (s32[128]{0:T(128)S(1)}, s32[128]{0:T(128)}, u32[]{:S(2)}) copy-start(s32[128]{0:T(128)} %param.11) | copy-start | bytes 1540

commit v7 on v6

--- a/solution.py
+++ b/solution.py
@@ -10,6 +10,13 @@
 AXES = ("dp", "split")
 NT = (((1,), (1,)), ((), ()))
 FAR = 1e9
+
+
+def plane_order(planes):
+    bits = max(planes.bit_length() - 1, 0)
+    if planes != 1 << bits:
+        return list(range(planes))
+    return [sum((z >> i & 1) << bits - 1 - i for i in range(bits)) for z in range(planes)]
 
 
 def iota(shape, dim):
@@ -42,7 +49,10 @@
     slot = jnp.dot(owner, named, preferred_element_type=jnp.float32)[0:1].astype(jnp.int32)
     core = lax.axis_index("dp") % 2
     here = jnp.where(slot % 2 == core, 1, 0)
-    target = jnp.where(member >= 0, (here * splits + rank // block) * chips + slot // 2, -1)
+    chip = jnp.zeros_like(slot)
+    for i, z in enumerate(plane_order(chips // splits)):
+        chip = jnp.where(slot // (2 * splits) == z, i * splits + slot // 2 % splits, chip)
+    target = jnp.where(member >= 0, (here * splits + rank // block) * chips + chip, -1)
     chosen = bf16(iota((2 * splits * chips, rows), 0) == target)
     high, low = (rank + 1) // 16, (rank + 1) % 16
     lane = iota((128, rows), 0)
@@ -177,8 +187,9 @@
         return ((z * splits + y) * 2 + core) * splits + x
 
     everywhere = [(z, a, b) for z in range(planes) for a in range(splits) for b in range(splits)]
-    columns = [[device(z, j, 0, g) for z in range(planes) for j in range(splits)] for g in range(splits)]
-    columns += [[device(z, g, 1, j) for z in range(planes) for j in range(splits)] for g in range(splits)]
+    order = plane_order(planes)
+    columns = [[device(z, j, 0, g) for z in order for j in range(splits)] for g in range(splits)]
+    columns += [[device(z, g, 1, j) for z in order for j in range(splits)] for g in range(splits)]
     sheets = [
         [device(z, a, core, b) for a in range(splits) for b in range(splits)] for z in range(planes) for core in range(2)
     ]

time: 107 us -> 107 us (level)
  the two profiles are of different devices: /device:TPU:2 before, /device:TPU:32 now
where the time goes in v7:
time: 107 us
  blocking collectives  74.6 us (70%)
  waiting for transfers between devices  13.7 us (13%)
  starting transfers between devices  8.72 us (8%)
  Pallas kernels  7.31 us (7%)
  other arithmetic  1.39 us (1%)
    all_to_all x1, blocking collectives, local(): lax.all_to_all(outgoing, AXES, 0, 0, tiled=True, axis_index_groups=columns)  64.5 us
    ppermute x2, waiting for transfers between devices, shift(): return lax.ppermute(array, AXES, pairs)  12 us
    all_to_all x1, blocking collectives, local(): lax.all_to_all(best, AXES, 0, 0, tiled=True, axis_index_groups=sheets)  10.1 us
    ppermute x2, starting transfers between devices, shift(): return lax.ppermute(array, AXES, pairs)  6.8 us
    pallas_call x1, Pallas kernels, local(): pl.pallas_call(lambda *refs: project_kernel(splits, block, *refs), out_sh...  3.45 us
  transfers between devices with their start and end apart: 3, of which 3 were waited for; matrix products, arithmetic and copies ran while one was open for 0% of the time, Pallas kernels for 1%

profile of v7, /device:TPU:32, one launch (start us, length us, event | category | flops | bytes accessed | tf_op | source)
XLA Modules:
  0.0 106.9 jit_solution(1807174070144512358)
XLA Ops:
  0.0 0.7 add_select_fusion
  0.7 0.0 copy-start
  0.7 0.7 copy-done
  1.4 3.5 %project.1 = (bf16[64,3200]{1,0:T(8,128)(2,1)S(1)}, bf16[64,3200]{1,0:T(8,128)(2,1)S(1)}) custom-call(bf16[512,1024]{1,0:T(8,128)(2,1)} %refs_0_.1, bf16[1024,768]{1,0:T(8,128)(2,1)} %refs_1_.1, s32[1,512]{1,0:T(1,128)S(1)} %bitcast.6, s32[1,128]{1,0:T(1,128)S(1)} %bitcast.7), custom_call_target="tpu_custom_call" | custom-call | tf_op jit(solution)/shard_map/project/pallas_call | solution.py:203
  4.8 1.9 %collective-permute-start = (bf16[64,3200]{1,0:T(8,128)(2,1)S(1)}, bf16[64,3200]{1,0:T(8,128)(2,1)S(1)}, u32[]{:S(2)}, u32[]{:S(2)}) collective-permute-start(bf16[64,3200]{1,0:T(8,128)(2,1)S(1)} %get-tuple-element.8), channel_id=1, source_target_pairs={{0,4},{4,0},{1,5},{5,1},{2,6},{6,2},{3,7},{7,3},{8,12},{12,8},{9,1... | collective-permute-start | bytes 1228808 | tf_op jit(solution)/shard_map/ppermute | solution.py:225
  6.7 1.7 %collective-permute-done.second_ref = bf16[64,3200]{1,0:T(8,128)(2,1)S(1)} collective-permute-done((bf16[64,3200]{1,0:T(8,128)(2,1)S(1)}, bf16[64,3200]{1,0:T(8,128)(2,1)S(1)}, u32[]{:S(2)}, u32[]{:S(2)}) %collective-permute-start) | collective-permute-done | bytes 409632 | tf_op jit(solution)/shard_map/ppermute | solution.py:225
  8.5 0.4 merge.1
  8.9 64.5 %all_to_all.10 = bf16[64,2,3200]{2,1,0:T(2,128)(2,1)S(1)} all-to-all(bf16[64,2,3200]{2,1,0:T(2,128)(2,1)S(1)} %merge.1), channel_id=1, replica_groups={{0,8,16,24,256,264,272,280,128,136,144,152,384,392,400,408,64,72,80,88,..., dimensions={0} | all-to-all | bytes 1638400 | tf_op jit(solution)/shard_map/all_to_all | solution.py:226
  73.4 0.3 reshape.16.refs_0_.refs_3_
  73.7 4.9 %collective-permute-start.2 = (bf16[128,3200]{1,0:T(8,128)(2,1)S(1)}, bf16[128,3200]{1,0:T(8,128)(2,1)S(1)}, u32[]{:S(2)}, u32[]{:S(2)}) collective-permute-start(bf16[128,3200]{1,0:T(8,128)(2,1)S(1)} %reshape.16.refs_0_.refs_3_), channel_id=1, source_target_pairs={{0,3},{1,0},{2,1},{3,2},{8,11},{9,8},{10,9},{11,10},{16,19},{17,16... | collective-permute-start | bytes 2457608 | tf_op jit(solution)/shard_map/ppermute | solution.py:200
  78.6 1.9 %collective-permute-start.1 = (bf16[128,3200]{1,0:T(8,128)(2,1)S(1)}, bf16[128,3200]{1,0:T(8,128)(2,1)S(1)}, u32[]{:S(2)}, u32[]{:S(2)}) collective-permute-start(bf16[128,3200]{1,0:T(8,128)(2,1)S(1)} %reshape.16.refs_0_.refs_3_), channel_id=1, source_target_pairs={{0,1},{1,2},{2,3},{3,0},{8,9},{9,10},{10,11},{11,8},{16,17},{17,18... | collective-permute-start | bytes 2457608 | tf_op jit(solution)/shard_map/ppermute | solution.py:200
  80.6 0.1 pad_add_fusion.refs_0_
  80.6 0.0 copy-start.1
  80.6 0.0 copy-start.2
  80.6 0.7 own.1.refs_2_
  81.3 7.1 %collective-permute-done.2.refs_1_.refs_5_ = bf16[128,3200]{1,0:T(8,128)(2,1)S(1)} collective-permute-done((bf16[128,3200]{1,0:T(8,128)(2,1)S(1)}, bf16[128,3200]{1,0:T(8,128)(2,1)S(1)}, u32[]{:S(2)}, u32[]{:S(2)}) %collective-permute-start.2) | collective-permute-done | bytes 819232 | tf_op jit(solution)/shard_map/ppermute | solution.py:200
  88.4 0.7 side.1.refs_6_
  89.1 4.9 %collective-permute-done.1.refs_4_ = bf16[128,3200]{1,0:T(8,128)(2,1)S(1)} collective-permute-done((bf16[128,3200]{1,0:T(8,128)(2,1)S(1)}, bf16[128,3200]{1,0:T(8,128)(2,1)S(1)}, u32[]{:S(2)}, u32[]{:S(2)}) %collective-permute-start.1) | collective-permute-done | bytes 819232 | tf_op jit(solution)/shard_map/ppermute | solution.py:200
  94.0 0.0 copy-done.1
  94.0 0.0 copy-done.2
  94.0 2.1 %ring.1 = f32[16,1,512]{2,1,0:T(1,128)S(1)} custom-call(s32[2]{0:T(128)S(1)} %pad_add_fusion.refs_0_, s32[1,128]{1,0:T(1,128)S(1)} %bitcast.8, s32[1,128]{1,0:T(1,128)S(1)} %bitcast.9, bf16[128,3200]{1,0:T(8,128)(2,1)S(1)} %reshape.16.refs_0_.refs_3_, bf16[128,3200]{1,0:T(8,128)(2,1)S(1)} %collective-permute-done.1.refs_4_, ...), custom_call_target="tpu_custom_call" | custom-call | tf_op jit(solution)/shard_map/ring/pallas_call | solution.py:251
  96.1 10.1 %all_to_all.11 = f32[16,1,512]{2,1,0:T(1,128)S(1)} all-to-all(f32[16,1,512]{2,1,0:T(1,128)S(1)} %ring.1), channel_id=1, replica_groups={{0,1,2,3,8,9,10,11,16,17,18,19,24,25,26,27},{4,5,6,7,12,13,14,15,20,21,..., dimensions={0} | all-to-all | bytes 65536 | tf_op jit(solution)/shard_map/all_to_all | solution.py:259
  106.2 0.6 reduce_max.11
Async XLA Ops:
  0.7 0.7 copy-start
  4.8 3.6 %collective-permute-start = (bf16[64,3200]{1,0:T(8,128)(2,1)S(1)}, bf16[64,3200]{1,0:T(8,128)(2,1)S(1)}, u32[]{:S(2)}, u32[]{:S(2)}) collective-permute-start(bf16[64,3200]{1,0:T(8,128)(2,1)S(1)} %get-tuple-element.8), channel_id=1, source_target_pairs={{0,4},{4,0},{1,5},{5,1},{2,6},{6,2},{3,7},{7,3},{8,12},{12,8},{9,1... | collective-permute-start | bytes 1228808 | tf_op jit(solution)/shard_map/ppermute | solution.py:225
  73.7 14.7 %collective-permute-start.2 = (bf16[128,3200]{1,0:T(8,128)(2,1)S(1)}, bf16[128,3200]{1,0:T(8,128)(2,1)S(1)}, u32[]{:S(2)}, u32[]{:S(2)}) collective-permute-start(bf16[128,3200]{1,0:T(8,128)(2,1)S(1)} %reshape.16.refs_0_.refs_3_), channel_id=1, source_target_pairs={{0,3},{1,0},{2,1},{3,2},{8,11},{9,8},{10,9},{11,10},{16,19},{17,16... | collective-permute-start | bytes 2457608 | tf_op jit(solution)/shard_map/ppermute | solution.py:200
  78.6 15.4 %collective-permute-start.1 = (bf16[128,3200]{1,0:T(8,128)(2,1)S(1)}, bf16[128,3200]{1,0:T(8,128)(2,1)S(1)}, u32[]{:S(2)}, u32[]{:S(2)}) collective-permute-start(bf16[128,3200]{1,0:T(8,128)(2,1)S(1)} %reshape.16.refs_0_.refs_3_), channel_id=1, source_target_pairs={{0,1},{1,2},{2,3},{3,0},{8,9},{9,10},{10,11},{11,8},{16,17},{17,18... | collective-permute-start | bytes 2457608 | tf_op jit(solution)/shard_map/ppermute | solution.py:200
  80.6 13.4 %copy-start.1 = (s32[128]{0:T(128)S(1)}, s32[128]{0:T(128)}, u32[]{:S(2)}) copy-start(s32[128]{0:T(128)} %param.10) | copy-start | bytes 1540
  80.6 13.4 %copy-start.2 = (s32[128]{0:T(128)S(1)}, s32[128]{0:T(128)}, u32[]{:S(2)}) copy-start(s32[128]{0:T(128)} %param.11) | copy-start | bytes 1540

commit v8 on v7

--- a/solution.py
+++ b/solution.py
@@ -27,9 +27,7 @@
     return mask_or_int.astype(jnp.float32).astype(jnp.bfloat16)
 
 
-def project_kernel(
-    splits, block, features_hbm, weight_hbm, member_ref, owner_ref, other_ref, mine_ref, features, weight, semaphores
-):
+def project_kernel(splits, block, features_hbm, weight_hbm, member_ref, owner_ref, out_ref, features, weight, semaphores):
     steps = 4
     part = features.shape[1] // steps
     spans = [slice(i * part, (i + 1) * part) for i in range(steps)]
@@ -42,26 +40,23 @@
         copy.start()
     member = member_ref[...]
     clusters, rows, width = owner_ref.shape[1], member.shape[1], weight.shape[1]
-    chips = mine_ref.shape[0]
+    lines = out_ref.shape[0]
     cluster, rank = member // TILE, member % TILE
     owner = bf16(jnp.broadcast_to(owner_ref[...], (8, clusters)))
     named = bf16(iota((clusters, rows), 0) == cluster)
     slot = jnp.dot(owner, named, preferred_element_type=jnp.float32)[0:1].astype(jnp.int32)
-    core = lax.axis_index("dp") % 2
-    here = jnp.where(slot % 2 == core, 1, 0)
-    chip = jnp.zeros_like(slot)
-    for i, z in enumerate(plane_order(chips // splits)):
-        chip = jnp.where(slot // (2 * splits) == z, i * splits + slot // 2 % splits, chip)
-    target = jnp.where(member >= 0, (here * splits + rank // block) * chips + chip, -1)
-    chosen = bf16(iota((2 * splits * chips, rows), 0) == target)
+    position = jnp.zeros_like(slot)
+    for i, z in enumerate(plane_order(clusters // (2 * splits))):
+        position = jnp.where(slot // (2 * splits) == z, i * (2 * splits) + slot % (2 * splits), position)
+    place = rank // block
+    target = jnp.where(member >= 0, place % 2 * lines + position * (splits // 2) + place // 2, -1)
+    chosen = bf16(iota((2 * lines, rows), 0) == target)
     high, low = (rank + 1) // 16, (rank + 1) % 16
     lane = iota((128, rows), 0)
-    digits = bf16(jnp.where(lane // 2 == rank // block, jnp.where(lane % 2 == 0, high, low), 0))
-    for i, out_ref in enumerate((other_ref, mine_ref)):
-        parts = [chosen[(i * splits + a) * chips : (i * splits + a + 1) * chips] for a in range(splits)]
-        anywhere = (parts[0] + parts[1]) + (parts[2] + parts[3])
-        numbers = lax.dot_general(anywhere, digits, NT, preferred_element_type=jnp.float32)
-        out_ref[:, splits * width :] = numbers.astype(jnp.bfloat16)
+    digits = bf16(jnp.where(lane // 2 == place % 2, jnp.where(lane % 2 == 0, high, low), 0))
+    anywhere = chosen[:lines] + chosen[lines:]
+    numbers = lax.dot_general(anywhere, digits, NT, preferred_element_type=jnp.float32)
+    out_ref[:, 2 * width :] = numbers.astype(jnp.bfloat16)
 
     projected = jnp.zeros((rows, width), jnp.float32)
     for i, span in enumerate(spans):
@@ -71,41 +66,37 @@
     normed = projected * lax.rsqrt(jnp.sum(projected * projected, axis=1, keepdims=True) + EPS)
     normed = normed.astype(jnp.bfloat16)
     sent = jnp.dot(chosen, normed, preferred_element_type=jnp.float32).astype(jnp.bfloat16)
-    for i, out_ref in enumerate((other_ref, mine_ref)):
-        for a in range(splits):
-            start = (i * splits + a) * chips
-            out_ref[:, a * width : (a + 1) * width] = sent[start : start + chips]
-
-
-def merge_kernel(first_ref, second_ref, out_ref):
-    out_ref[:, 0, :] = first_ref[...]
-    out_ref[:, 1, :] = second_ref[...]
+    for i in range(2):
+        out_ref[:, i * width : (i + 1) * width] = sent[i * lines : (i + 1) * lines]
 
 
 class Members:
     def __init__(self, ref, width, splits):
-        self.ref, self.width, self.splits, self.digits = ref, width, splits, ref[:, splits * width :]
+        self.ref, self.width, self.splits, self.digits = ref, width, splits, ref[:, 2 * width :]
+        self.step = ref.shape[0] // 2
 
     def rows(self, index):
-        return self.ref[:, index * self.width : (index + 1) * self.width]
+        span = slice(index // 2 * self.step, (index // 2 + 1) * self.step)
+        return self.ref[span, index % 2 * self.width : (index % 2 + 1) * self.width]
 
     def down(self):
-        step = self.ref.shape[0]
-        lane, digit = iota((128, self.splits * step), 1) // step, iota((128, self.splits * step), 0)
+        lane, digit = iota((128, 2 * self.step), 1) // self.step, iota((128, 2 * self.step), 0)
         weights = bf16(jnp.where(digit == 2 * lane, 16, jnp.where(digit == 2 * lane + 1, 1, 0)))
-        return jnp.dot(self.digits, weights, preferred_element_type=jnp.float32)
+        found = jnp.dot(self.digits, weights, preferred_element_type=jnp.float32)
+        return jnp.concatenate([found[: self.step], found[self.step :]], axis=1)
 
     def along(self):
         line, digit = iota((8, 128), 0), iota((8, 128), 1)
         weights = bf16(jnp.where(digit == 2 * line, 16, jnp.where(digit == 2 * line + 1, 1, 0)))
-        return lax.dot_general(weights, self.digits, NT, preferred_element_type=jnp.float32)
+        found = lax.dot_general(weights, self.digits, NT, preferred_element_type=jnp.float32)
+        return jnp.concatenate([found[0:2, : self.step], found[0:2, self.step :]], axis=0)
 
     def stacked(self):
         return jnp.concatenate([self.rows(a) for a in range(self.splits)], axis=0)
 
 
 def earlier_max(best, members, queries):
-    splits, step = len(best), queries.ref.shape[0]
+    splits, step = len(best), queries.step
     later, numbers = queries.stacked(), queries.along()
     for part in members:
         scores = lax.dot_general(part.stacked(), later, NT, preferred_element_type=jnp.float32)
@@ -187,9 +178,10 @@
         return ((z * splits + y) * 2 + core) * splits + x
 
     everywhere = [(z, a, b) for z in range(planes) for a in range(splits) for b in range(splits)]
-    order = plane_order(planes)
-    columns = [[device(z, j, 0, g) for z in order for j in range(splits)] for g in range(splits)]
-    columns += [[device(z, g, 1, j) for z in order for j in range(splits)] for g in range(splits)]
+    crosses = [
+        [device(z, g, 1, j) if core else device(z, j, 0, g) for z in plane_order(planes) for j in range(splits) for core in range(2)]
+        for g in range(splits)
+    ]
     sheets = [
         [device(z, a, core, b) for a in range(splits) for b in range(splits)] for z in range(planes) for core in range(2)
     ]
@@ -199,12 +191,11 @@
         pairs += [(device(z, a, 1, b), device(z, (a + step) % splits, 1, b)) for z, a, b in everywhere]
         return lax.ppermute(array, AXES, pairs)
 
-    chips = owners // 2
-    other, mine = pl.pallas_call(
+    outgoing = pl.pallas_call(
         lambda *refs: project_kernel(splits, block, *refs),
-        out_shape=[jax.ShapeDtypeStruct((chips, splits * width + 128), jnp.bfloat16)] * 2,
+        out_shape=jax.ShapeDtypeStruct((rows // 2, 2 * width + 128), jnp.bfloat16),
         in_specs=[hbm] * 2 + [vmem] * 2,
-        out_specs=[vmem] * 2,
+        out_specs=vmem,
         scratch_shapes=[
             pltpu.VMEM(features.shape, jnp.bfloat16),
             pltpu.VMEM(proj_weight.shape, jnp.bfloat16),
@@ -214,16 +205,10 @@
         name="project",
     )(features, proj_weight, member.reshape(1, rows), owner_row)
 
-    swap = [(device(z, a, core, b), device(z, a, 1 - core, b)) for z, a, b in everywhere for core in range(2)]
-    outgoing = pl.pallas_call(
-        merge_kernel,
-        out_shape=jax.ShapeDtypeStruct((chips, 2, splits * width + 128), jnp.bfloat16),
-        in_specs=[vmem] * 2,
-        out_specs=vmem,
-        compiler_params=params,
-        name="merge",
-    )(mine, lax.ppermute(other, AXES, swap))
-    own = lax.all_to_all(outgoing, AXES, 0, 0, tiled=True, axis_index_groups=columns).reshape(owners, -1)
+    own = lax.all_to_all(
+        outgoing.reshape(owners, splits // 2, -1), AXES, 0, 0, tiled=True, axis_index_groups=crosses
+    )
+    own = own.transpose(1, 0, 2).reshape(rows // 2, -1)
     left, right = shift(own, 1), shift(own, -1)
 
     best = pl.pallas_call(

time: 107 us -> 106 us (level)
  blocking collectives: 74.6 us -> 76.2 us
  waiting for transfers between devices: 13.7 us -> 12.4 us
    ppermute x1 -> x0, starting transfers between devices: 1.92 us -> none  [local(): lax.ppermute(other, AXES, swap)]
    ppermute x1 -> x0, waiting for transfers between devices: 1.71 us -> none  [local(): lax.ppermute(other, AXES, swap)]
    all_to_all x1, blocking collectives: 64.5 us -> 66 us  [local(): lax.all_to_all(outgoing.reshape(owners, splits // 2, -1), AXES, 0, 0, til...]
  transfers between devices with their start and end apart: 3 -> 2, of which waited for: 3 -> 2; matrix products, arithmetic and copies ran while one was open for 0% -> 0% of each run, Pallas kernels for 1% -> 1%
where the time goes in v8:
time: 106 us
  blocking collectives  76.2 us (72%)
  waiting for transfers between devices  12.4 us (12%)
  starting transfers between devices  7.86 us (7%)
  Pallas kernels  6.86 us (6%)
  other arithmetic  1.39 us (1%)
  local copies, waits for them, and re-layouts  1.07 us (1%)
    all_to_all x1, blocking collectives, local(): lax.all_to_all(outgoing.reshape(owners, splits // 2, -1), AXES, 0, 0, til...  66 us
    ppermute x2, waiting for transfers between devices, shift(): return lax.ppermute(array, AXES, pairs)  12.4 us
    all_to_all x1, blocking collectives, local(): lax.all_to_all(best, AXES, 0, 0, tiled=True, axis_index_groups=sheets)  10.1 us
    ppermute x2, starting transfers between devices, shift(): return lax.ppermute(array, AXES, pairs)  7.86 us
    pallas_call x1, Pallas kernels, local(): pl.pallas_call(lambda *refs: project_kernel(splits, block, *refs), out_sh...  3.51 us
  transfers between devices with their start and end apart: 2, of which 2 were waited for; matrix products, arithmetic and copies ran while one was open for 0% of the time, Pallas kernels for 1%

profile of v8, /device:TPU:32, one launch (start us, length us, event | category | flops | bytes accessed | tf_op | source)
XLA Modules:
  0.0 105.8 jit_solution(1059385063554598664)
XLA Ops:
  0.0 0.7 add_select_fusion
  0.7 0.0 copy-start
  0.7 0.7 copy-done
  1.4 3.5 %project.1 = bf16[256,1664]{1,0:T(8,128)(2,1)S(1)} custom-call(bf16[512,1024]{1,0:T(8,128)(2,1)} %refs_0_.1, bf16[1024,768]{1,0:T(8,128)(2,1)} %refs_1_.1, s32[1,512]{1,0:T(1,128)S(1)} %bitcast.13, s32[1,128]{1,0:T(1,128)S(1)} %bitcast.14), custom_call_target="tpu_custom_call" | custom-call | tf_op jit(solution)/shard_map/project/pallas_call | solution.py:194
  4.9 0.3 reshape.19
  5.2 66.0 %all_to_all.10 = bf16[128,2,1664]{2,1,0:T(2,128)(2,1)S(1)} all-to-all(bf16[128,2,1664]{2,1,0:T(2,128)(2,1)S(1)} %reshape.19), channel_id=1, replica_groups={{0,4,8,5,16,6,24,7,256,260,264,261,272,262,280,263,128,132,136,133,144,..., dimensions={0} | all-to-all | bytes 1703936 | tf_op jit(solution)/shard_map/all_to_all | solution.py:208
  71.2 0.1 copy.8
  71.3 5.9 %collective-permute-start.1 = (bf16[256,1664]{1,0:T(8,128)(2,1)S(1)}, bf16[256,1664]{1,0:T(8,128)(2,1)S(1)}, u32[]{:S(2)}, u32[]{:S(2)}) collective-permute-start(bf16[256,1664]{1,0:T(8,128)(2,1)S(1)} %bitcast.8), channel_id=1, source_target_pairs={{0,3},{1,0},{2,1},{3,2},{8,11},{9,8},{10,9},{11,10},{16,19},{17,16... | collective-permute-start | bytes 2555912 | tf_op jit(solution)/shard_map/ppermute | solution.py:192
  77.3 1.9 %collective-permute-start = (bf16[256,1664]{1,0:T(8,128)(2,1)S(1)}, bf16[256,1664]{1,0:T(8,128)(2,1)S(1)}, u32[]{:S(2)}, u32[]{:S(2)}) collective-permute-start(bf16[256,1664]{1,0:T(8,128)(2,1)S(1)} %bitcast.9), channel_id=1, source_target_pairs={{0,1},{1,2},{2,3},{3,0},{8,9},{9,10},{10,11},{11,8},{16,17},{17,18... | collective-permute-start | bytes 2555912 | tf_op jit(solution)/shard_map/ppermute | solution.py:192
  79.2 0.1 pad_add_fusion.refs_0_
  79.3 0.0 copy-start.1
  79.3 0.0 copy-start.2
  79.3 0.7 own.1.refs_2_
  80.0 7.5 %collective-permute-done.1.refs_1_.refs_5_ = bf16[256,1664]{1,0:T(8,128)(2,1)S(1)} collective-permute-done((bf16[256,1664]{1,0:T(8,128)(2,1)S(1)}, bf16[256,1664]{1,0:T(8,128)(2,1)S(1)}, u32[]{:S(2)}, u32[]{:S(2)}) %collective-permute-start.1) | collective-permute-done | bytes 852000 | tf_op jit(solution)/shard_map/ppermute | solution.py:192
  87.5 0.7 side.1.refs_6_
  88.1 4.9 %collective-permute-done.refs_4_ = bf16[256,1664]{1,0:T(8,128)(2,1)S(1)} collective-permute-done((bf16[256,1664]{1,0:T(8,128)(2,1)S(1)}, bf16[256,1664]{1,0:T(8,128)(2,1)S(1)}, u32[]{:S(2)}, u32[]{:S(2)}) %collective-permute-start) | collective-permute-done | bytes 852000 | tf_op jit(solution)/shard_map/ppermute | solution.py:192
  93.1 0.0 copy-done.1
  93.1 0.0 copy-done.2
  93.1 2.0 %ring.1 = f32[16,1,512]{2,1,0:T(1,128)S(1)} custom-call(s32[2]{0:T(128)S(1)} %pad_add_fusion.refs_0_, s32[1,128]{1,0:T(1,128)S(1)} %bitcast.15, s32[1,128]{1,0:T(1,128)S(1)} %bitcast.16, bf16[256,1664]{1,0:T(8,128)(2,1)S(1)} %bitcast.12, bf16[256,1664]{1,0:T(8,128)(2,1)S(1)} %collective-permute-done.refs_4_, ...), custom_call_target="tpu_custom_call" | custom-call | tf_op jit(solution)/shard_map/ring/pallas_call | solution.py:236
  95.1 10.1 %all_to_all.11 = f32[16,1,512]{2,1,0:T(1,128)S(1)} all-to-all(f32[16,1,512]{2,1,0:T(1,128)S(1)} %ring.1), channel_id=1, replica_groups={{0,1,2,3,8,9,10,11,16,17,18,19,24,25,26,27},{4,5,6,7,12,13,14,15,20,21,..., dimensions={0} | all-to-all | bytes 65536 | tf_op jit(solution)/shard_map/all_to_all | solution.py:244
  105.2 0.6 reduce_max.11
Async XLA Ops:
  0.7 0.7 copy-start
  71.3 16.1 %collective-permute-start.1 = (bf16[256,1664]{1,0:T(8,128)(2,1)S(1)}, bf16[256,1664]{1,0:T(8,128)(2,1)S(1)}, u32[]{:S(2)}, u32[]{:S(2)}) collective-permute-start(bf16[256,1664]{1,0:T(8,128)(2,1)S(1)} %bitcast.8), channel_id=1, source_target_pairs={{0,3},{1,0},{2,1},{3,2},{8,11},{9,8},{10,9},{11,10},{16,19},{17,16... | collective-permute-start | bytes 2555912 | tf_op jit(solution)/shard_map/ppermute | solution.py:192
  77.3 15.8 %collective-permute-start = (bf16[256,1664]{1,0:T(8,128)(2,1)S(1)}, bf16[256,1664]{1,0:T(8,128)(2,1)S(1)}, u32[]{:S(2)}, u32[]{:S(2)}) collective-permute-start(bf16[256,1664]{1,0:T(8,128)(2,1)S(1)} %bitcast.9), channel_id=1, source_target_pairs={{0,1},{1,2},{2,3},{3,0},{8,9},{9,10},{10,11},{11,8},{16,17},{17,18... | collective-permute-start | bytes 2555912 | tf_op jit(solution)/shard_map/ppermute | solution.py:192
  79.3 13.7 %copy-start.1 = (s32[128]{0:T(128)S(1)}, s32[128]{0:T(128)}, u32[]{:S(2)}) copy-start(s32[128]{0:T(128)} %param.10) | copy-start | bytes 1540
  79.3 13.7 %copy-start.2 = (s32[128]{0:T(128)S(1)}, s32[128]{0:T(128)}, u32[]{:S(2)}) copy-start(s32[128]{0:T(128)} %param.11) | copy-start | bytes 1540

commit v9 on v8

--- a/solution.py
+++ b/solution.py
@@ -130,7 +130,7 @@
     block = out_ref.shape[2]
     own, left, right = [Members(ref, width, splits) for ref in (own_ref, left_ref, right_ref)]
     own_best = [best_ref[:, a * step : (a + 1) * step] for a in range(splits)]
-    own_best = earlier_max(own_best, [left], own)
+    own_best = earlier_max(own_best, [right], own)
     left_best = [jnp.full((8, step), -1.0, jnp.float32) for _ in range(splits)]
     left_best = earlier_max(left_best, [right], left)
     own_down, left_down = own.down(), left.down()
@@ -228,7 +228,7 @@
         compiler_params=params,
         name="side",
         cost_estimate=pl.CostEstimate(flops=2 * rows * rows * width, bytes_accessed=2 << 20, transcendentals=0),
-    )(own, right, best)
+    )(own, left, best)
     owner, x = lax.axis_index("dp"), lax.axis_index("split")
     z, y, core = owner // (2 * splits), owner // 2 % splits, owner % 2
     line = jnp.where(core == 0, y, x)

time: 106 us -> 106 us (level)
  waiting for transfers between devices: 12.4 us -> 8.69 us
  blocking collectives: 76.2 us -> 79.4 us
    ppermute x2, waiting for transfers between devices: 12.4 us -> 8.69 us  [shift(): return lax.ppermute(array, AXES, pairs)]
    all_to_all x1, blocking collectives: 10.1 us -> 13.4 us  [local(): lax.all_to_all(best, AXES, 0, 0, tiled=True, axis_index_groups=sheets)]
where the time goes in v9:
time: 106 us; the launch traced here: 105 us
  blocking collectives  79.4 us (75%)
  waiting for transfers between devices  8.69 us (8%)
  starting transfers between devices  7.86 us (7%)
  Pallas kernels  6.82 us (6%)
  other arithmetic  1.39 us (1%)
  local copies, waits for them, and re-layouts  1.07 us (1%)
    all_to_all x1, blocking collectives, local(): lax.all_to_all(outgoing.reshape(owners, splits // 2, -1), AXES, 0, 0, til...  66 us
    all_to_all x1, blocking collectives, local(): lax.all_to_all(best, AXES, 0, 0, tiled=True, axis_index_groups=sheets)  13.4 us
    ppermute x2, waiting for transfers between devices, shift(): return lax.ppermute(array, AXES, pairs)  8.69 us
    ppermute x2, starting transfers between devices, shift(): return lax.ppermute(array, AXES, pairs)  7.86 us
    pallas_call x1, Pallas kernels, local(): pl.pallas_call(lambda *refs: project_kernel(splits, block, *refs), out_sh...  3.51 us
  transfers between devices with their start and end apart: 2, of which 2 were waited for; matrix products, arithmetic and copies ran while one was open for 0% of the time, Pallas kernels for 1%

profile of v9, /device:TPU:32, one launch (start us, length us, event | category | flops | bytes accessed | tf_op | source)
XLA Modules:
  0.0 105.3 jit_solution(9523276943323160810)
XLA Ops:
  0.0 0.7 add_select_fusion
  0.7 0.0 copy-start
  0.7 0.7 copy-done
  1.4 3.5 %project.1 = bf16[256,1664]{1,0:T(8,128)(2,1)S(1)} custom-call(bf16[512,1024]{1,0:T(8,128)(2,1)} %refs_0_.1, bf16[1024,768]{1,0:T(8,128)(2,1)} %refs_1_.1, s32[1,512]{1,0:T(1,128)S(1)} %bitcast.13, s32[1,128]{1,0:T(1,128)S(1)} %bitcast.14), custom_call_target="tpu_custom_call" | custom-call | tf_op jit(solution)/shard_map/project/pallas_call | solution.py:194
  4.9 0.3 reshape.19
  5.2 66.0 %all_to_all.10 = bf16[128,2,1664]{2,1,0:T(2,128)(2,1)S(1)} all-to-all(bf16[128,2,1664]{2,1,0:T(2,128)(2,1)S(1)} %reshape.19), channel_id=1, replica_groups={{0,4,8,5,16,6,24,7,256,260,264,261,272,262,280,263,128,132,136,133,144,..., dimensions={0} | all-to-all | bytes 1703936 | tf_op jit(solution)/shard_map/all_to_all | solution.py:208
  71.2 0.1 copy.8
  71.3 2.9 %collective-permute-start = (bf16[256,1664]{1,0:T(8,128)(2,1)S(1)}, bf16[256,1664]{1,0:T(8,128)(2,1)S(1)}, u32[]{:S(2)}, u32[]{:S(2)}) collective-permute-start(bf16[256,1664]{1,0:T(8,128)(2,1)S(1)} %bitcast.8), channel_id=1, source_target_pairs={{0,1},{1,2},{2,3},{3,0},{8,9},{9,10},{10,11},{11,8},{16,17},{17,18... | collective-permute-start | bytes 2555912 | tf_op jit(solution)/shard_map/ppermute | solution.py:192
  74.2 5.0 %collective-permute-start.1 = (bf16[256,1664]{1,0:T(8,128)(2,1)S(1)}, bf16[256,1664]{1,0:T(8,128)(2,1)S(1)}, u32[]{:S(2)}, u32[]{:S(2)}) collective-permute-start(bf16[256,1664]{1,0:T(8,128)(2,1)S(1)} %bitcast.9), channel_id=1, source_target_pairs={{0,3},{1,0},{2,1},{3,2},{8,11},{9,8},{10,9},{11,10},{16,19},{17,16... | collective-permute-start | bytes 2555912 | tf_op jit(solution)/shard_map/ppermute | solution.py:192
  79.2 0.1 pad_add_fusion.refs_0_
  79.3 0.0 copy-start.1
  79.3 0.0 copy-start.2
  79.3 0.7 own.1.refs_2_
  80.0 7.9 %collective-permute-done.refs_1_.refs_4_ = bf16[256,1664]{1,0:T(8,128)(2,1)S(1)} collective-permute-done((bf16[256,1664]{1,0:T(8,128)(2,1)S(1)}, bf16[256,1664]{1,0:T(8,128)(2,1)S(1)}, u32[]{:S(2)}, u32[]{:S(2)}) %collective-permute-start) | collective-permute-done | bytes 852000 | tf_op jit(solution)/shard_map/ppermute | solution.py:192
  87.9 0.7 side.1.refs_6_
  88.6 0.8 collective-permute-done.1.refs_5_
  89.4 0.0 copy-done.1
  89.4 0.0 copy-done.2
  89.4 2.0 %ring.1 = f32[16,1,512]{2,1,0:T(1,128)S(1)} custom-call(s32[2]{0:T(128)S(1)} %pad_add_fusion.refs_0_, s32[1,128]{1,0:T(1,128)S(1)} %bitcast.15, s32[1,128]{1,0:T(1,128)S(1)} %bitcast.16, bf16[256,1664]{1,0:T(8,128)(2,1)S(1)} %bitcast.12, bf16[256,1664]{1,0:T(8,128)(2,1)S(1)} %collective-permute-done.refs_1_.refs_4_, ...), custom_call_target="tpu_custom_call" | custom-call | tf_op jit(solution)/shard_map/ring/pallas_call | solution.py:236
  91.4 13.4 %all_to_all.11 = f32[16,1,512]{2,1,0:T(1,128)S(1)} all-to-all(f32[16,1,512]{2,1,0:T(1,128)S(1)} %ring.1), channel_id=1, replica_groups={{0,1,2,3,8,9,10,11,16,17,18,19,24,25,26,27},{4,5,6,7,12,13,14,15,20,21,..., dimensions={0} | all-to-all | bytes 65536 | tf_op jit(solution)/shard_map/all_to_all | solution.py:244
  104.7 0.6 reduce_max.11
Async XLA Ops:
  0.7 0.7 copy-start
  71.3 16.6 %collective-permute-start = (bf16[256,1664]{1,0:T(8,128)(2,1)S(1)}, bf16[256,1664]{1,0:T(8,128)(2,1)S(1)}, u32[]{:S(2)}, u32[]{:S(2)}) collective-permute-start(bf16[256,1664]{1,0:T(8,128)(2,1)S(1)} %bitcast.8), channel_id=1, source_target_pairs={{0,1},{1,2},{2,3},{3,0},{8,9},{9,10},{10,11},{11,8},{16,17},{17,18... | collective-permute-start | bytes 2555912 | tf_op jit(solution)/shard_map/ppermute | solution.py:192
  74.2 15.2 %collective-permute-start.1 = (bf16[256,1664]{1,0:T(8,128)(2,1)S(1)}, bf16[256,1664]{1,0:T(8,128)(2,1)S(1)}, u32[]{:S(2)}, u32[]{:S(2)}) collective-permute-start(bf16[256,1664]{1,0:T(8,128)(2,1)S(1)} %bitcast.9), channel_id=1, source_target_pairs={{0,3},{1,0},{2,1},{3,2},{8,11},{9,8},{10,9},{11,10},{16,19},{17,16... | collective-permute-start | bytes 2555912 | tf_op jit(solution)/shard_map/ppermute | solution.py:192
  79.3 10.1 %copy-start.1 = (s32[128]{0:T(128)S(1)}, s32[128]{0:T(128)}, u32[]{:S(2)}) copy-start(s32[128]{0:T(128)} %param.10) | copy-start | bytes 1540
  79.3 10.1 %copy-start.2 = (s32[128]{0:T(128)S(1)}, s32[128]{0:T(128)}, u32[]{:S(2)}) copy-start(s32[128]{0:T(128)} %param.11) | copy-start | bytes 1540

commit v10 on v9

--- a/solution.py
+++ b/solution.py
@@ -16,7 +16,7 @@
     bits = max(planes.bit_length() - 1, 0)
     if planes != 1 << bits:
         return list(range(planes))
-    return [sum((z >> i & 1) << bits - 1 - i for i in range(bits)) for z in range(planes)]
+    return [sum((z >> i & 1) << bits - 1 - i for i in range(bits)) for z in range(planes)][::-1]
 
 
 def iota(shape, dim):

time: 106 us -> 104 us (0.981)
  the two profiles are of different devices: /device:TPU:32 before, /device:TPU:64 now
where the time goes in v10:
time: 104 us
  blocking collectives  76.4 us (73%)
  waiting for transfers between devices  9.44 us (9%)
  starting transfers between devices  8.37 us (8%)
  Pallas kernels  6.82 us (7%)
  other arithmetic  1.39 us (1%)
  local copies, waits for them, and re-layouts  1.07 us (1%)
    all_to_all x1, blocking collectives, local(): lax.all_to_all(outgoing.reshape(owners, splits // 2, -1), AXES, 0, 0, til...  60.8 us
    all_to_all x1, blocking collectives, local(): lax.all_to_all(best, AXES, 0, 0, tiled=True, axis_index_groups=sheets)  15.5 us
    ppermute x2, waiting for transfers between devices, shift(): return lax.ppermute(array, AXES, pairs)  9.44 us
    ppermute x2, starting transfers between devices, shift(): return lax.ppermute(array, AXES, pairs)  8.37 us
    pallas_call x1, Pallas kernels, local(): pl.pallas_call(lambda *refs: project_kernel(splits, block, *refs), out_sh...  3.51 us
  transfers between devices with their start and end apart: 2, of which 2 were waited for; matrix products, arithmetic and copies ran while one was open for 0% of the time, Pallas kernels for 1%

profile of v10, /device:TPU:64, one launch (start us, length us, event | category | flops | bytes accessed | tf_op | source)
XLA Modules:
  0.0 103.6 jit_solution(13007448503935073238)
XLA Ops:
  0.0 0.7 add_select_fusion
  0.7 0.0 copy-start
  0.7 0.7 copy-done
  1.4 3.5 %project.1 = bf16[256,1664]{1,0:T(8,128)(2,1)S(1)} custom-call(bf16[512,1024]{1,0:T(8,128)(2,1)} %refs_0_.1, bf16[1024,768]{1,0:T(8,128)(2,1)} %refs_1_.1, s32[1,512]{1,0:T(1,128)S(1)} %bitcast.13, s32[1,128]{1,0:T(1,128)S(1)} %bitcast.14), custom_call_target="tpu_custom_call" | custom-call | tf_op jit(solution)/shard_map/project/pallas_call | solution.py:194
  4.9 0.3 reshape.19
  5.2 60.8 %all_to_all.10 = bf16[128,2,1664]{2,1,0:T(2,128)(2,1)S(1)} all-to-all(bf16[128,2,1664]{2,1,0:T(2,128)(2,1)S(1)} %reshape.19), channel_id=1, replica_groups={{480,484,488,485,496,486,504,487,224,228,232,229,240,230,248,231,352,35..., dimensions={0} | all-to-all | bytes 1703936 | tf_op jit(solution)/shard_map/all_to_all | solution.py:208
  66.0 0.1 copy.8
  66.1 4.3 %collective-permute-start = (bf16[256,1664]{1,0:T(8,128)(2,1)S(1)}, bf16[256,1664]{1,0:T(8,128)(2,1)S(1)}, u32[]{:S(2)}, u32[]{:S(2)}) collective-permute-start(bf16[256,1664]{1,0:T(8,128)(2,1)S(1)} %bitcast.8), channel_id=1, source_target_pairs={{0,1},{1,2},{2,3},{3,0},{8,9},{9,10},{10,11},{11,8},{16,17},{17,18... | collective-permute-start | bytes 2555912 | tf_op jit(solution)/shard_map/ppermute | solution.py:192
  70.4 4.1 %collective-permute-start.1 = (bf16[256,1664]{1,0:T(8,128)(2,1)S(1)}, bf16[256,1664]{1,0:T(8,128)(2,1)S(1)}, u32[]{:S(2)}, u32[]{:S(2)}) collective-permute-start(bf16[256,1664]{1,0:T(8,128)(2,1)S(1)} %bitcast.9), channel_id=1, source_target_pairs={{0,3},{1,0},{2,1},{3,2},{8,11},{9,8},{10,9},{11,10},{16,19},{17,16... | collective-permute-start | bytes 2555912 | tf_op jit(solution)/shard_map/ppermute | solution.py:192
  74.6 0.1 pad_add_fusion.refs_0_
  74.6 0.0 copy-start.1
  74.6 0.0 copy-start.2
  74.6 0.7 own.1.refs_2_
  75.3 7.9 %collective-permute-done.refs_1_.refs_4_ = bf16[256,1664]{1,0:T(8,128)(2,1)S(1)} collective-permute-done((bf16[256,1664]{1,0:T(8,128)(2,1)S(1)}, bf16[256,1664]{1,0:T(8,128)(2,1)S(1)}, u32[]{:S(2)}, u32[]{:S(2)}) %collective-permute-start) | collective-permute-done | bytes 852000 | tf_op jit(solution)/shard_map/ppermute | solution.py:192
  83.2 0.7 side.1.refs_6_
  83.9 1.5 %collective-permute-done.1.refs_5_ = bf16[256,1664]{1,0:T(8,128)(2,1)S(1)} collective-permute-done((bf16[256,1664]{1,0:T(8,128)(2,1)S(1)}, bf16[256,1664]{1,0:T(8,128)(2,1)S(1)}, u32[]{:S(2)}, u32[]{:S(2)}) %collective-permute-start.1) | collective-permute-done | bytes 852000 | tf_op jit(solution)/shard_map/ppermute | solution.py:192
  85.5 0.0 copy-done.1
  85.5 0.0 copy-done.2
  85.5 2.0 %ring.1 = f32[16,1,512]{2,1,0:T(1,128)S(1)} custom-call(s32[2]{0:T(128)S(1)} %pad_add_fusion.refs_0_, s32[1,128]{1,0:T(1,128)S(1)} %bitcast.15, s32[1,128]{1,0:T(1,128)S(1)} %bitcast.16, bf16[256,1664]{1,0:T(8,128)(2,1)S(1)} %bitcast.12, bf16[256,1664]{1,0:T(8,128)(2,1)S(1)} %collective-permute-done.refs_1_.refs_4_, ...), custom_call_target="tpu_custom_call" | custom-call | tf_op jit(solution)/shard_map/ring/pallas_call | solution.py:236
  87.4 15.5 %all_to_all.11 = f32[16,1,512]{2,1,0:T(1,128)S(1)} all-to-all(f32[16,1,512]{2,1,0:T(1,128)S(1)} %ring.1), channel_id=1, replica_groups={{0,1,2,3,8,9,10,11,16,17,18,19,24,25,26,27},{4,5,6,7,12,13,14,15,20,21,..., dimensions={0} | all-to-all | bytes 65536 | tf_op jit(solution)/shard_map/all_to_all | solution.py:244
  103.0 0.6 reduce_max.11
Async XLA Ops:
  0.7 0.7 copy-start
  66.1 17.1 %collective-permute-start = (bf16[256,1664]{1,0:T(8,128)(2,1)S(1)}, bf16[256,1664]{1,0:T(8,128)(2,1)S(1)}, u32[]{:S(2)}, u32[]{:S(2)}) collective-permute-start(bf16[256,1664]{1,0:T(8,128)(2,1)S(1)} %bitcast.8), channel_id=1, source_target_pairs={{0,1},{1,2},{2,3},{3,0},{8,9},{9,10},{10,11},{11,8},{16,17},{17,18... | collective-permute-start | bytes 2555912 | tf_op jit(solution)/shard_map/ppermute | solution.py:192
  70.4 15.1 %collective-permute-start.1 = (bf16[256,1664]{1,0:T(8,128)(2,1)S(1)}, bf16[256,1664]{1,0:T(8,128)(2,1)S(1)}, u32[]{:S(2)}, u32[]{:S(2)}) collective-permute-start(bf16[256,1664]{1,0:T(8,128)(2,1)S(1)} %bitcast.9), channel_id=1, source_target_pairs={{0,3},{1,0},{2,1},{3,2},{8,11},{9,8},{10,9},{11,10},{16,19},{17,16... | collective-permute-start | bytes 2555912 | tf_op jit(solution)/shard_map/ppermute | solution.py:192
  74.6 10.8 %copy-start.1 = (s32[128]{0:T(128)S(1)}, s32[128]{0:T(128)}, u32[]{:S(2)}) copy-start(s32[128]{0:T(128)} %param.10) | copy-start | bytes 1540
  74.6 10.8 %copy-start.2 = (s32[128]{0:T(128)S(1)}, s32[128]{0:T(128)}, u32[]{:S(2)}) copy-start(s32[128]{0:T(128)} %param.11) | copy-start | bytes 1540

commit v11 on v10

--- a/solution.py
+++ b/solution.py
@@ -159,7 +159,7 @@
         ordered = found[0:1] + found[1:2] + found[2:3]
         ordered = jnp.where((found[3:4] > 0) & (rank < size), ordered, -1.0)
         for i in range(splits):
-            out_ref[i * splits + a] = jnp.where(index_ref[1] == i, ordered, -1.0)
+            out_ref[splits * splits - 1 - (i * splits + a)] = jnp.where(index_ref[1] == i, ordered, -1.0)
 
 
 def local(features, proj_weight, row_cluster, row_rank, owner_slot, tile_size):
@@ -183,7 +183,7 @@
         for g in range(splits)
     ]
     sheets = [
-        [device(z, a, core, b) for a in range(splits) for b in range(splits)] for z in range(planes) for core in range(2)
+        [device(z, a, core, b) for a in range(splits) for b in range(splits)][::-1] for z in range(planes) for core in range(2)
     ]
 
     def shift(array, step):

time: 104 us -> 104 us (level)
  the two profiles are of different devices: /device:TPU:64 before, /device:TPU:32 now
where the time goes in v11:
time: 104 us; the launch traced here: 103 us
  blocking collectives  74.3 us (71%)
  starting transfers between devices  10 us (10%)
  waiting for transfers between devices  9.66 us (9%)
  Pallas kernels  6.82 us (7%)
  other arithmetic  1.39 us (1%)
  local copies, waits for them, and re-layouts  1.07 us (1%)
    all_to_all x1, blocking collectives, local(): lax.all_to_all(outgoing.reshape(owners, splits // 2, -1), AXES, 0, 0, til...  62.3 us
    all_to_all x1, blocking collectives, local(): lax.all_to_all(best, AXES, 0, 0, tiled=True, axis_index_groups=sheets)  12 us
    ppermute x2, starting transfers between devices, shift(): return lax.ppermute(array, AXES, pairs)  10 us
    ppermute x2, waiting for transfers between devices, shift(): return lax.ppermute(array, AXES, pairs)  9.66 us
    pallas_call x1, Pallas kernels, local(): pl.pallas_call(lambda *refs: project_kernel(splits, block, *refs), out_sh...  3.51 us
  transfers between devices with their start and end apart: 2, of which 2 were waited for; matrix products, arithmetic and copies ran while one was open for 0% of the time, Pallas kernels for 1%

profile of v11, /device:TPU:32, one launch (start us, length us, event | category | flops | bytes accessed | tf_op | source)
XLA Modules:
  0.0 103.4 jit_solution(3074866205588809870)
XLA Ops:
  0.0 0.7 add_select_fusion
  0.7 0.0 copy-start
  0.7 0.7 copy-done
  1.4 3.5 %project.1 = bf16[256,1664]{1,0:T(8,128)(2,1)S(1)} custom-call(bf16[512,1024]{1,0:T(8,128)(2,1)} %refs_0_.1, bf16[1024,768]{1,0:T(8,128)(2,1)} %refs_1_.1, s32[1,512]{1,0:T(1,128)S(1)} %bitcast.13, s32[1,128]{1,0:T(1,128)S(1)} %bitcast.14), custom_call_target="tpu_custom_call" | custom-call | tf_op jit(solution)/shard_map/project/pallas_call | solution.py:194
  4.9 0.3 reshape.19
  5.2 62.3 %all_to_all.10 = bf16[128,2,1664]{2,1,0:T(2,128)(2,1)S(1)} all-to-all(bf16[128,2,1664]{2,1,0:T(2,128)(2,1)S(1)} %reshape.19), channel_id=1, replica_groups={{480,484,488,485,496,486,504,487,224,228,232,229,240,230,248,231,352,35..., dimensions={0} | all-to-all | bytes 1703936 | tf_op jit(solution)/shard_map/all_to_all | solution.py:208
  67.5 0.1 copy.8
  67.6 6.6 %collective-permute-start = (bf16[256,1664]{1,0:T(8,128)(2,1)S(1)}, bf16[256,1664]{1,0:T(8,128)(2,1)S(1)}, u32[]{:S(2)}, u32[]{:S(2)}) collective-permute-start(bf16[256,1664]{1,0:T(8,128)(2,1)S(1)} %bitcast.8), channel_id=1, source_target_pairs={{0,1},{1,2},{2,3},{3,0},{8,9},{9,10},{10,11},{11,8},{16,17},{17,18... | collective-permute-start | bytes 2555912 | tf_op jit(solution)/shard_map/ppermute | solution.py:192
  74.2 3.4 %collective-permute-start.1 = (bf16[256,1664]{1,0:T(8,128)(2,1)S(1)}, bf16[256,1664]{1,0:T(8,128)(2,1)S(1)}, u32[]{:S(2)}, u32[]{:S(2)}) collective-permute-start(bf16[256,1664]{1,0:T(8,128)(2,1)S(1)} %bitcast.9), channel_id=1, source_target_pairs={{0,3},{1,0},{2,1},{3,2},{8,11},{9,8},{10,9},{11,10},{16,19},{17,16... | collective-permute-start | bytes 2555912 | tf_op jit(solution)/shard_map/ppermute | solution.py:192
  77.7 0.1 pad_add_fusion.refs_0_
  77.8 0.0 copy-start.1
  77.8 0.0 copy-start.2
  77.8 0.7 own.1.refs_2_
  78.5 7.9 %collective-permute-done.refs_1_.refs_4_ = bf16[256,1664]{1,0:T(8,128)(2,1)S(1)} collective-permute-done((bf16[256,1664]{1,0:T(8,128)(2,1)S(1)}, bf16[256,1664]{1,0:T(8,128)(2,1)S(1)}, u32[]{:S(2)}, u32[]{:S(2)}) %collective-permute-start) | collective-permute-done | bytes 852000 | tf_op jit(solution)/shard_map/ppermute | solution.py:192
  86.4 0.7 side.1.refs_6_
  87.1 1.7 %collective-permute-done.1.refs_5_ = bf16[256,1664]{1,0:T(8,128)(2,1)S(1)} collective-permute-done((bf16[256,1664]{1,0:T(8,128)(2,1)S(1)}, bf16[256,1664]{1,0:T(8,128)(2,1)S(1)}, u32[]{:S(2)}, u32[]{:S(2)}) %collective-permute-start.1) | collective-permute-done | bytes 852000 | tf_op jit(solution)/shard_map/ppermute | solution.py:192
  88.8 0.0 copy-done.1
  88.8 0.0 copy-done.2
  88.8 2.0 %ring.1 = f32[16,1,512]{2,1,0:T(1,128)S(1)} custom-call(s32[2]{0:T(128)S(1)} %pad_add_fusion.refs_0_, s32[1,128]{1,0:T(1,128)S(1)} %bitcast.15, s32[1,128]{1,0:T(1,128)S(1)} %bitcast.16, bf16[256,1664]{1,0:T(8,128)(2,1)S(1)} %bitcast.12, bf16[256,1664]{1,0:T(8,128)(2,1)S(1)} %collective-permute-done.refs_1_.refs_4_, ...), custom_call_target="tpu_custom_call" | custom-call | tf_op jit(solution)/shard_map/ring/pallas_call | solution.py:236
  90.8 12.0 %all_to_all.11 = f32[16,1,512]{2,1,0:T(1,128)S(1)} all-to-all(f32[16,1,512]{2,1,0:T(1,128)S(1)} %ring.1), channel_id=1, replica_groups={{27,26,25,24,19,18,17,16,11,10,9,8,3,2,1,0},{31,30,29,28,23,22,21,20,15..., dimensions={0} | all-to-all | bytes 65536 | tf_op jit(solution)/shard_map/all_to_all | solution.py:244
  102.7 0.6 reduce_max.11
Async XLA Ops:
  0.7 0.7 copy-start
  67.6 18.8 %collective-permute-start = (bf16[256,1664]{1,0:T(8,128)(2,1)S(1)}, bf16[256,1664]{1,0:T(8,128)(2,1)S(1)}, u32[]{:S(2)}, u32[]{:S(2)}) collective-permute-start(bf16[256,1664]{1,0:T(8,128)(2,1)S(1)} %bitcast.8), channel_id=1, source_target_pairs={{0,1},{1,2},{2,3},{3,0},{8,9},{9,10},{10,11},{11,8},{16,17},{17,18... | collective-permute-start | bytes 2555912 | tf_op jit(solution)/shard_map/ppermute | solution.py:192
  74.2 14.6 %collective-permute-start.1 = (bf16[256,1664]{1,0:T(8,128)(2,1)S(1)}, bf16[256,1664]{1,0:T(8,128)(2,1)S(1)}, u32[]{:S(2)}, u32[]{:S(2)}) collective-permute-start(bf16[256,1664]{1,0:T(8,128)(2,1)S(1)} %bitcast.9), channel_id=1, source_target_pairs={{0,3},{1,0},{2,1},{3,2},{8,11},{9,8},{10,9},{11,10},{16,19},{17,16... | collective-permute-start | bytes 2555912 | tf_op jit(solution)/shard_map/ppermute | solution.py:192
  77.8 11.0 %copy-start.1 = (s32[128]{0:T(128)S(1)}, s32[128]{0:T(128)}, u32[]{:S(2)}) copy-start(s32[128]{0:T(128)} %param.10) | copy-start | bytes 1540
  77.8 11.0 %copy-start.2 = (s32[128]{0:T(128)S(1)}, s32[128]{0:T(128)}, u32[]{:S(2)}) copy-start(s32[128]{0:T(128)} %param.11) | copy-start | bytes 1540
